TPU v7x, 512 devices: a whole 4x8x8 slice. The times are simulated.
512 devices in a mesh: gx: 32 (over x_lo, y, core), gy: 16 (over z, x_hi).
Axes of the slice: x: 4 (x_hi: 2, x_lo: 2; x = x_hi * 2 + x_lo), y: 8, z: 8, core: 2. Of those that a mesh axis runs over, the one named last changes fastest.
Arguments:
- features: bfloat16 [32, 16, 1, 512, 128], P('gx', 'gy'), may hold values from -6 to 6
- occupancy: int32 [32, 16, 1, 512], P('gx', 'gy'), may hold values from 0 to 1, as said below
- neighbours: int32 [32, 16, 1, 27], P('gx', 'gy'), may hold values from 0 to 9, as said below
- weight_sub: bfloat16 [27, 128, 128], replicated, may hold values from -0.109375 to 0.109375
- weight_down: bfloat16 [8, 128, 256], replicated, may hold values from -0.1875 to 0.1875
- cotangent: bfloat16 [32, 16, 1, 64, 256], P('gx', 'gy'), may hold values from -6 to 6
Outputs:
- output: bfloat16 [32, 16, 1, 64, 256], P('gx', 'gy')
- grad_features: bfloat16 [32, 16, 1, 512, 128], P('gx', 'gy')
- grad_sub: float32 [27, 128, 128], replicated
- grad_down: float32 [8, 128, 256], replicated
Inputs may be any that keep to these rules, and one draw needn't show every extreme that they name: `occupancy`: 0 or 1; every voxel of an empty slot is 0. `neighbours`: tile (x, y) covers the block cells (2 x + a, 2 y + b, c) with a, b, c in 0 and 1. Its single slot holds one active block of these cells. Entry k of an active block's list names the active block at block offset d_k as r + s, with s that block's slot and r = 3 (dx + 1) + (dy + 1) for its tile's offset (dx, dy); 9 where that cell holds no active block, and everywhere in an empty slot.
All inputs are finite; a program needn't handle non-finite values.
Results may differ from a plain program's by a relative error of at most 0.0049.
Values may be sent and summed in bfloat16 or wider, within the bound.
A program may use at most 64 MiB of HBM per device.

v0:
```python
import math

import jax
import jax.numpy as jnp
import numpy as np
from jax import lax
from jax.sharding import PartitionSpec as P

C1 = 128
C2 = 256
BS = 8
NB = 1
V = 512


def padded(block, sides, width):
    for axis, dim in sides:
        count = lax.axis_size(axis)
        forward = [(i, i + 1) for i in range(count - 1)]
        backward = [(target, source) for source, target in forward]
        low = lax.ppermute(
            lax.slice_in_dim(block, block.shape[dim] - width, None, axis=dim), axis, forward
        )
        high = lax.ppermute(lax.slice_in_dim(block, 0, width, axis=dim), axis, backward)
        block = jnp.concatenate([low, block, high], axis=dim)
    return block


def shifted(value, axis, steps):
    count = lax.axis_size(axis)
    first, last = (max(0, -steps), min(count, count - steps))
    return lax.ppermute(value, axis, [(source, source + steps) for source in range(first, last)])


def densify(block_pool, near_links):
    extent = block_pool.shape[1]
    source_spans = ((extent - 1, extent), (0, extent), (0, 1))
    planes = []
    for i in range(3):
        slab_rows = []
        for j in range(3):
            strips = []
            for l in range(3):
                region = block_pool[
                    :,
                    source_spans[i][0] : source_spans[i][1],
                    source_spans[j][0] : source_spans[j][1],
                    source_spans[l][0] : source_spans[l][1],
                    :,
                ]
                strips.append(jnp.take(region, near_links[:, 9 * i + 3 * j + l], axis=0))
            slab_rows.append(jnp.concatenate(strips, axis=3))
        planes.append(jnp.concatenate(slab_rows, axis=2))
    return jnp.concatenate(planes, axis=1)


def convolve(padded_field, weights):
    channels = padded_field.shape[-1]
    kernel = weights.reshape(3, 3, 3, channels, weights.shape[2])
    summed = lax.conv_general_dilated(
        padded_field,
        kernel,
        (1, 1, 1),
        "VALID",
        dimension_numbers=("NDHWC", "DHWIO", "NDHWC"),
        preferred_element_type=jnp.float32,
    )
    return summed.reshape(-1, weights.shape[2])


def weight_grads(padded_field, preact_grad):
    channels = padded_field.shape[-1]
    grads_field = preact_grad.reshape(NB, BS, BS, BS, preact_grad.shape[-1])
    terms = lax.conv_general_dilated(
        padded_field,
        grads_field,
        (1, 1, 1),
        "VALID",
        dimension_numbers=("CDHWN", "IDHWO", "NDHWC"),
        preferred_element_type=jnp.float32,
    )
    return jnp.transpose(terms, (1, 2, 3, 0, 4)).reshape(27, channels, preact_grad.shape[-1])


def with_blank(flat_pool):
    shaped = flat_pool.reshape(flat_pool.shape[0], BS, BS, BS, flat_pool.shape[-1])
    blank_block = jnp.zeros((1, BS, BS, BS, flat_pool.shape[-1]), flat_pool.dtype)
    return jnp.concatenate([shaped, blank_block], axis=0)


def group_children(hidden):
    half = BS // 2
    shaped = hidden.reshape(NB, half, 2, half, 2, half, 2, hidden.shape[-1])
    return jnp.transpose(shaped, (0, 1, 3, 5, 2, 4, 6, 7)).reshape(
        NB * half**3, 8 * hidden.shape[-1]
    )


def spread_children(grouped):
    half = BS // 2
    shaped = grouped.reshape(NB, half, half, half, 2, 2, 2, C1)
    return jnp.transpose(shaped, (0, 1, 4, 2, 5, 3, 6, 7)).reshape(NB * V, C1)


def coarse_mask(occupied):
    half = BS // 2
    return jnp.max(occupied.reshape(NB, half, 2, half, 2, half, 2), axis=(2, 4, 6)).reshape(
        NB * half**3, 1
    )


def scatter_back(beside_all, near_links):
    places = np.arange(BS + 2) - 1
    block_step = places // BS + 1
    inner_cell = places % BS
    offset_table = (
        block_step[:, None, None] * 9 + block_step[None, :, None] * 3 + block_step[None, None, :]
    ).reshape(-1)
    voxel_table = (
        inner_cell[:, None, None] * BS * BS
        + inner_cell[None, :, None] * BS
        + inner_cell[None, None, :]
    ).reshape(-1)
    chosen = jnp.take(near_links, jnp.asarray(offset_table, dtype=jnp.int32), axis=1)
    targets = chosen * V + jnp.asarray(voxel_table, dtype=jnp.int32)[None, :]
    pool_grads = jnp.zeros(((9 * NB + 1) * V, C1), jnp.float32)
    pool_grads = pool_grads.at[targets.reshape(-1)].add(beside_all.reshape(-1, C1))
    return pool_grads[: 9 * NB * V]


def local(features, occupancy, neighbours, weight_sub, weight_down, cotangent):
    near_links = neighbours[0, 0]
    occupied = occupancy[0, 0]
    live_mask = occupied.reshape(NB * V, 1).astype(jnp.float32)
    masked = features * occupancy[..., None].astype(jnp.bfloat16)
    neighbourhood = padded(masked, (("gx", 0), ("gy", 1)), 1)
    block_pool = with_blank(neighbourhood.reshape(9 * NB, V, C1))
    padded_field = densify(block_pool, near_links)
    preact = convolve(padded_field, weight_sub)
    hidden = (jax.nn.silu(preact) * live_mask).astype(jnp.bfloat16)
    grouped = group_children(hidden)
    coarse = coarse_mask(occupied)
    down_flat = weight_down.reshape(8 * C1, C2)
    output = (
        jnp.dot(grouped, down_flat, preferred_element_type=jnp.float32) * coarse.astype(jnp.float32)
    ).astype(jnp.bfloat16)
    seeded = cotangent[0, 0].reshape(NB * V // 8, C2) * coarse.astype(jnp.bfloat16)
    grad_down = lax.dot_general(
        grouped, seeded, (((0,), (0,)), ((), ())), preferred_element_type=jnp.float32
    ).reshape(8, C1, C2)
    hidden_grad = spread_children(
        lax.dot_general(
            seeded, down_flat, (((1,), (1,)), ((), ())), preferred_element_type=jnp.float32
        )
    )
    sigmoid_pre = jax.nn.sigmoid(preact)
    slopes = sigmoid_pre * (1.0 + preact * (1.0 - sigmoid_pre))
    preact_grad = (hidden_grad * slopes * live_mask).astype(jnp.bfloat16)
    grad_sub = weight_grads(padded_field, preact_grad)
    flipped = jnp.transpose(weight_sub[::-1], (0, 2, 1))
    spread_grad = jnp.pad(
        preact_grad.reshape(NB, BS, BS, BS, C1), ((0, 0), (2, 2), (2, 2), (2, 2), (0, 0))
    )
    beside_all = convolve(spread_grad, flipped).reshape(NB, (BS + 2) ** 3, C1)
    pool_grads = scatter_back(beside_all, near_links).reshape(3, 3, NB, V, C1)
    column_sum = pool_grads[:, 1]
    for shift_by, column in ((-1, 0), (1, 2)):
        column_sum = column_sum + shifted(
            pool_grads[:, column].astype(jnp.bfloat16), "gy", shift_by
        ).astype(jnp.float32)
    summed = column_sum[1]
    for shift_by, column in ((-1, 0), (1, 2)):
        summed = summed + shifted(column_sum[column].astype(jnp.bfloat16), "gx", shift_by).astype(
            jnp.float32
        )
    summed = summed.reshape(NB * V, C1)
    grad_features = (summed * live_mask).astype(jnp.bfloat16).reshape(1, 1, NB, V, C1)
    grad_sub, grad_down = lax.psum((grad_sub, grad_down), ("gx", "gy"))
    grad_scale = 1.0 / math.sqrt(lax.axis_size("gx") * lax.axis_size("gy") * NB * V)
    return (
        output.reshape(1, 1, NB, V // 8, C2),
        grad_features,
        grad_sub * grad_scale,
        grad_down * grad_scale,
    )


def solution(mesh):
    return jax.shard_map(
        local,
        mesh=mesh,
        in_specs=(
            P("gx", "gy", None, None, None),
            P("gx", "gy", None, None),
            P("gx", "gy", None, None),
            P(),
            P(),
            P("gx", "gy", None, None, None),
        ),
        out_specs=(P("gx", "gy", None, None, None), P("gx", "gy", None, None, None), P(), P()),
        check_vma=False,
    )
```

profile of v0, /device:TPU:1, one launch (start us, length us, event | category | flops | bytes accessed | tf_op | source)
XLA Modules:
  0.0 450.1 jit_solution(14456910327963095383)
XLA Ops:
  8.0 1.0 bitcast_multiply_fusion
  9.1 8.8 %collective-permute-start.1 = (bf16[1,1,1,512,128]{4,3,1,0,2:T(8,128)(2,1)S(1)}, bf16[1,1,1,512,128]{4,3,1,0,2:T(8,128)(2,1)S(1)}, u32[]{:S(2)}, u32[]{:S(2)}) collective-permute-start(bf16[1,1,1,512,128]{4,3,1,0,2:T(8,128)(2,1)S(1)} %bitcast_multiply_fusion), channel_id=1, source_target_pairs={{16,0},{32,16},{48,32},{64,48},{80,64},{96,80},{112,96},{128,112},... | collective-permute-start | bytes 393224 | tf_op jit(solution)/shard_map/ppermute | solution.py:24
  17.9 1.9 collective-permute-start
  19.8 2.1 fusion.31
  21.9 1.6 fusion.32
  23.5 1.6 fusion.30
  25.6 1.4 fusion.28
  27.7 0.8 broadcast_multiply_fusion.2
  30.6 1.3 collective-permute-start.3
  31.9 6.3 %collective-permute-start.2 = (bf16[3,1,1,512,128]{4,3,1,0,2:T(8,128)(2,1)}, bf16[3,1,1,512,128]{4,3,1,0,2:T(8,128)(2,1)}, u32[]{:S(2)}, u32[]{:S(2)}) collective-permute-start(bf16[3,1,1,512,128]{4,3,1,0,2:T(8,128)(2,1)} %pad_maximum_fusion.1), channel_id=1, source_target_pairs={{0,1},{1,2},{2,3},{3,4},{4,5},{5,6},{6,7},{7,8},{8,9},{9,10},{10,1... | collective-permute-start | bytes 1179656 | tf_op jit(solution)/shard_map/ppermute | solution.py:21
  89.1 1.1 copy.40
  90.2 0.8 copy.42
  92.4 17.2 %compare_select_fusion = s32[1000]{0:T(1024)S(1)} fusion(s32[1000]{0:T(1024)S(1)} %copy-done.9, pred[1000]{0:T(1024)(128)(4,1)S(1)} %copy-done.10, pred[1000]{0:T(1024)(128)(4,1)S(1)} %copy-done.11, pred[1000]{0:T(1024)(128)(4,1)S(1)} %copy-done.12, pred[1000]{0:T(1024)(128)(4,1)S(1)} %copy-done.13, pred[1000]{0:T(1024)(128)(4,1)S(1)} %copy-done.14, ...), kind=kLoop, calls=%fused_computation.45 | loop fusion | flops 31000 | bytes 34108 | tf_op jit(solution)/shard_map/select_n | solution.py:127
  109.6 1.1 pad_maximum_fusion
  110.8 1.5 copy.37
  113.9 8.4 %maximum_maximum_fusion = bf16[1,10,10,10,128]{4,0,3,2,1:T(2,128)(2,1)S(1)} fusion(bf16[1,1,1,1,128]{4,0,3,2,1:T(2,128)(2,1)S(1)} %get-tuple-element.193, bf16[1,1,1,8,128]{4,0,3,2,1:T(2,128)(2,1)S(1)} %get-tuple-element.201, bf16[1,1,1,1,128]{4,0,3,2,1:T(2,128)(2,1)S(1)} %get-tuple-element.194, bf16[1,1,8,1,128]{4,0,3,2,1:T(2,128)(2,1)S(1)} %get-tuple-element.205, ...), kind=kLoop, calls=%fused_computation.14 | loop fusion | flops 3328000 | bytes 512000 | tf_op jit(solution)/shard_map/concatenate | solution.py:54
  122.3 4.5 %multiply_convert_fusion = (bf16[1,8,8,8,128]{4,0,3,2,1:T(2,128)(2,1)}, f32[1,8,8,8,128]{4,0,3,2,1:T(1,128)S(1)}) fusion(f32[1,8,8,8,128]{4,0,3,2,1:T(1,128)S(1)} %bitcast.218, f32[8,8,8]{2,1,0:T(8,128)S(1)} %convert_element_type.150, bf16[1,10,10,10,128]{4,0,3,2,1:T(2,128)(2,1)S(1)} %maximum_maximum_fusion, bf16[3,3,3,128,128]{4,3,2,1,0:T(8,128)(2,1)S(1)} %bitcast.215), kind=kOutput, calls=%fused_computation.25 | convolution fusion | flops 453640192 | bytes 1798144 | tf_op jit(solution)/shard_map/conv_general_dilated | solution.py:60
  127.2 6.0 %fusion.34 = f32[3,3,3,128,128]{4,3,2,1,0:T(8,128)} fusion(bf16[1,10,10,10,128]{4,0,3,2,1:T(2,128)(2,1)S(1)} %maximum_maximum_fusion, bf16[1,8,8,8,128]{4,0,3,2,1:T(2,128)(2,1)} %get-tuple-element.191), kind=kOutput, calls=%fused_computation.103 | convolution fusion | flops 452984832 | bytes 2156544 | tf_op jit(solution)/shard_map/transpose | solution.py:82
  133.3 5.8 %fusion.33 = f32[1,10,10,10,128]{4,0,3,2,1:T(1,128)S(1)} fusion(bf16[1,8,8,8,128]{4,0,3,2,1:T(2,128)(2,1)S(1)} %copy-done.36, bf16[3,3,3,128,128]{3,4,2,1,0:T(8,128)(2,1)S(1)} %bitcast.216), kind=kOutput, calls=%fused_computation.102 | convolution fusion | flops 452984832 | bytes 1527808 | tf_op jit(solution)/shard_map/conv_general_dilated | solution.py:60
  139.0 7.8 %scatter_custom_fusion = f32[5120,128]{1,0:T(8,128)} fusion(s32[1000]{0:T(1024)S(1)} %compare_select_fusion, f32[1000,128]{1,0:T(8,128)S(1)} %bitcast.220, f32[]{:T(128)} %constant.101.clone.1), kind=kCustom, calls=%fused_computation.1 | custom fusion | flops 128000 | bytes 2621444 | tf_op jit(solution)/shard_map/scatter-add | solution.py:127
  146.9 1.8 slice.404
  149.7 2.0 collective-permute-start.5
  151.7 1.3 collective-permute-start.4
  153.0 1.3 fusion.13
  154.4 12.9 %collective-permute-done.5 = bf16[3,1,512,128]{3,2,0,1:T(8,128)(2,1)} collective-permute-done((bf16[3,1,512,128]{3,2,0,1:T(8,128)(2,1)}, bf16[3,1,512,128]{3,2,0,1:T(8,128)(2,1)}, u32[]{:S(2)}, u32[]{:S(2)}) %collective-permute-start.5) | collective-permute-done | bytes 393248 | tf_op jit(solution)/shard_map/ppermute | solution.py:32
  167.4 1.2 fusion.11
  168.6 4.1 collective-permute-start.7
  172.7 1.9 collective-permute-start.6
  175.5 3.9 collective-permute-done.6
  180.2 259.0 %all-reduce.4.cloned.1.call-done = (f32[27,128,128]{2,1,0:T(8,128)}, f32[8,128,256]{2,1,0:T(8,128)}) async-done(((f32[27,128,128]{2,1,0:T(8,128)}, f32[8,128,256]{2,1,0:T(8,128)}), (f32[27,128,128]{2,1,0:T(8,128)}, f32[8,128,256]{2,1,0:T(8,128)})) %all-reduce.4.cloned.1.call-update) | async-done | bytes 2818064 | tf_op jit(solution)/shard_map/psum | solution.py:178
  439.2 3.0 broadcast_multiply_fusion
  442.2 1.1 broadcast_multiply_fusion.1
  (126 shorter events, 9.5 us)
Async XLA Ops:
  7.2 84.0 %copy-start.3 = (bf16[27,128,128]{2,1,0:T(8,128)(2,1)S(1)}, bf16[27,128,128]{2,1,0:T(8,128)(2,1)}, u32[]{:S(2)}) copy-start(bf16[27,128,128]{2,1,0:T(8,128)(2,1)} %param.25) | copy-start | bytes 2654212
  7.2 432.0 %all-reduce.4.cloned.1.call-start = ((), (), s32[]{:S(2)}) async-start(), calls=%async_computation | async-start | bytes 5636096 | tf_op jit(solution)/shard_map/psum | solution.py:178
  9.1 20.8 %collective-permute-start.1 = (bf16[1,1,1,512,128]{4,3,1,0,2:T(8,128)(2,1)S(1)}, bf16[1,1,1,512,128]{4,3,1,0,2:T(8,128)(2,1)S(1)}, u32[]{:S(2)}, u32[]{:S(2)}) collective-permute-start(bf16[1,1,1,512,128]{4,3,1,0,2:T(8,128)(2,1)S(1)} %bitcast_multiply_fusion), channel_id=1, source_target_pairs={{16,0},{32,16},{48,32},{64,48},{80,64},{96,80},{112,96},{128,112},... | collective-permute-start | bytes 393224 | tf_op jit(solution)/shard_map/ppermute | solution.py:24
  17.9 12.0 %collective-permute-start = (bf16[1,1,1,512,128]{4,3,1,0,2:T(8,128)(2,1)S(1)}, bf16[1,1,1,512,128]{4,3,1,0,2:T(8,128)(2,1)S(1)}, u32[]{:S(2)}, u32[]{:S(2)}) collective-permute-start(bf16[1,1,1,512,128]{4,3,1,0,2:T(8,128)(2,1)S(1)} %bitcast_multiply_fusion), channel_id=1, source_target_pairs={{0,16},{16,32},{32,48},{48,64},{64,80},{80,96},{96,112},{112,128},... | collective-permute-start | bytes 393224 | tf_op jit(solution)/shard_map/ppermute | solution.py:21
  29.5 62.7 %copy-start.9 = (s32[1000]{0:T(1024)S(1)}, s32[1000]{0:T(1024)}, u32[]{:S(2)}) copy-start(s32[1000]{0:T(1024)} %constant.431) | copy-start | bytes 12004
  29.5 62.7 %copy-start.10 = (pred[1000]{0:T(1024)(128)(4,1)S(1)}, pred[1000]{0:T(1024)(128)(4,1)}, u32[]{:S(2)}) copy-start(pred[1000]{0:T(1024)(128)(4,1)} %constant.403) | copy-start | bytes 3004
  29.5 62.7 %copy-start.11 = (pred[1000]{0:T(1024)(128)(4,1)S(1)}, pred[1000]{0:T(1024)(128)(4,1)}, u32[]{:S(2)}) copy-start(pred[1000]{0:T(1024)(128)(4,1)} %constant.404) | copy-start | bytes 3004
  29.5 62.7 %copy-start.12 = (pred[1000]{0:T(1024)(128)(4,1)S(1)}, pred[1000]{0:T(1024)(128)(4,1)}, u32[]{:S(2)}) copy-start(pred[1000]{0:T(1024)(128)(4,1)} %constant.405) | copy-start | bytes 3004
  29.5 62.6 %copy-start.13 = (pred[1000]{0:T(1024)(128)(4,1)S(1)}, pred[1000]{0:T(1024)(128)(4,1)}, u32[]{:S(2)}) copy-start(pred[1000]{0:T(1024)(128)(4,1)} %constant.406) | copy-start | bytes 3004
  29.6 62.6 %copy-start.14 = (pred[1000]{0:T(1024)(128)(4,1)S(1)}, pred[1000]{0:T(1024)(128)(4,1)}, u32[]{:S(2)}) copy-start(pred[1000]{0:T(1024)(128)(4,1)} %constant.407) | copy-start | bytes 3004
  29.6 62.6 %copy-start.15 = (pred[1000]{0:T(1024)(128)(4,1)S(1)}, pred[1000]{0:T(1024)(128)(4,1)}, u32[]{:S(2)}) copy-start(pred[1000]{0:T(1024)(128)(4,1)} %constant.408) | copy-start | bytes 3004
  29.6 62.6 %copy-start.16 = (pred[1000]{0:T(1024)(128)(4,1)S(1)}, pred[1000]{0:T(1024)(128)(4,1)}, u32[]{:S(2)}) copy-start(pred[1000]{0:T(1024)(128)(4,1)} %constant.409) | copy-start | bytes 3004
  29.6 62.6 %copy-start.17 = (pred[1000]{0:T(1024)(128)(4,1)S(1)}, pred[1000]{0:T(1024)(128)(4,1)}, u32[]{:S(2)}) copy-start(pred[1000]{0:T(1024)(128)(4,1)} %constant.410) | copy-start | bytes 3004
  29.6 62.6 %copy-start.18 = (pred[1000]{0:T(1024)(128)(4,1)S(1)}, pred[1000]{0:T(1024)(128)(4,1)}, u32[]{:S(2)}) copy-start(pred[1000]{0:T(1024)(128)(4,1)} %constant.411) | copy-start | bytes 3004
  29.6 62.6 %copy-start.19 = (pred[1000]{0:T(1024)(128)(4,1)S(1)}, pred[1000]{0:T(1024)(128)(4,1)}, u32[]{:S(2)}) copy-start(pred[1000]{0:T(1024)(128)(4,1)} %constant.412) | copy-start | bytes 3004
  29.6 62.6 %copy-start.20 = (pred[1000]{0:T(1024)(128)(4,1)S(1)}, pred[1000]{0:T(1024)(128)(4,1)}, u32[]{:S(2)}) copy-start(pred[1000]{0:T(1024)(128)(4,1)} %constant.413) | copy-start | bytes 3004
  29.6 62.6 %copy-start.21 = (pred[1000]{0:T(1024)(128)(4,1)S(1)}, pred[1000]{0:T(1024)(128)(4,1)}, u32[]{:S(2)}) copy-start(pred[1000]{0:T(1024)(128)(4,1)} %constant.414) | copy-start | bytes 3004
  29.7 62.6 %copy-start.22 = (pred[1000]{0:T(1024)(128)(4,1)S(1)}, pred[1000]{0:T(1024)(128)(4,1)}, u32[]{:S(2)}) copy-start(pred[1000]{0:T(1024)(128)(4,1)} %constant.415) | copy-start | bytes 3004
  29.7 62.6 %copy-start.23 = (pred[1000]{0:T(1024)(128)(4,1)S(1)}, pred[1000]{0:T(1024)(128)(4,1)}, u32[]{:S(2)}) copy-start(pred[1000]{0:T(1024)(128)(4,1)} %constant.416) | copy-start | bytes 3004
  29.7 62.6 %copy-start.24 = (pred[1000]{0:T(1024)(128)(4,1)S(1)}, pred[1000]{0:T(1024)(128)(4,1)}, u32[]{:S(2)}) copy-start(pred[1000]{0:T(1024)(128)(4,1)} %constant.417) | copy-start | bytes 3004
  29.7 62.6 %copy-start.25 = (pred[1000]{0:T(1024)(128)(4,1)S(1)}, pred[1000]{0:T(1024)(128)(4,1)}, u32[]{:S(2)}) copy-start(pred[1000]{0:T(1024)(128)(4,1)} %constant.418) | copy-start | bytes 3004
  29.7 62.6 %copy-start.26 = (pred[1000]{0:T(1024)(128)(4,1)S(1)}, pred[1000]{0:T(1024)(128)(4,1)}, u32[]{:S(2)}) copy-start(pred[1000]{0:T(1024)(128)(4,1)} %constant.419) | copy-start | bytes 3004
  29.7 62.6 %copy-start.27 = (pred[1000]{0:T(1024)(128)(4,1)S(1)}, pred[1000]{0:T(1024)(128)(4,1)}, u32[]{:S(2)}) copy-start(pred[1000]{0:T(1024)(128)(4,1)} %constant.420) | copy-start | bytes 3004
  29.7 62.6 %copy-start.28 = (pred[1000]{0:T(1024)(128)(4,1)S(1)}, pred[1000]{0:T(1024)(128)(4,1)}, u32[]{:S(2)}) copy-start(pred[1000]{0:T(1024)(128)(4,1)} %constant.421) | copy-start | bytes 3004
  29.7 62.6 %copy-start.29 = (pred[1000]{0:T(1024)(128)(4,1)S(1)}, pred[1000]{0:T(1024)(128)(4,1)}, u32[]{:S(2)}) copy-start(pred[1000]{0:T(1024)(128)(4,1)} %constant.422) | copy-start | bytes 3004
  29.8 62.6 %copy-start.30 = (pred[1000]{0:T(1024)(128)(4,1)S(1)}, pred[1000]{0:T(1024)(128)(4,1)}, u32[]{:S(2)}) copy-start(pred[1000]{0:T(1024)(128)(4,1)} %constant.423) | copy-start | bytes 3004
  30.6 79.0 %collective-permute-start.3 = (bf16[3,1,1,512,128]{4,3,1,0,2:T(8,128)(2,1)}, bf16[3,1,1,512,128]{4,3,1,0,2:T(8,128)(2,1)S(1)}, u32[]{:S(2)}, u32[]{:S(2)}) collective-permute-start(bf16[3,1,1,512,128]{4,3,1,0,2:T(8,128)(2,1)} %pad_maximum_fusion.1), channel_id=1, source_target_pairs={{1,0},{2,1},{3,2},{4,3},{5,4},{6,5},{7,6},{8,7},{9,8},{10,9},{11,1... | collective-permute-start | bytes 1179656 | tf_op jit(solution)/shard_map/ppermute | solution.py:24
  31.9 77.7 %collective-permute-start.2 = (bf16[3,1,1,512,128]{4,3,1,0,2:T(8,128)(2,1)}, bf16[3,1,1,512,128]{4,3,1,0,2:T(8,128)(2,1)}, u32[]{:S(2)}, u32[]{:S(2)}) collective-permute-start(bf16[3,1,1,512,128]{4,3,1,0,2:T(8,128)(2,1)} %pad_maximum_fusion.1), channel_id=1, source_target_pairs={{0,1},{1,2},{2,3},{3,4},{4,5},{5,6},{6,7},{7,8},{8,9},{9,10},{10,1... | collective-permute-start | bytes 1179656 | tf_op jit(solution)/shard_map/ppermute | solution.py:21
  149.7 17.7 %collective-permute-start.5 = (bf16[3,1,512,128]{3,2,0,1:T(8,128)(2,1)}, bf16[3,1,512,128]{3,2,0,1:T(8,128)(2,1)}, u32[]{:S(2)}, u32[]{:S(2)}) collective-permute-start(bf16[3,1,512,128]{3,2,0,1:T(8,128)(2,1)} %get-tuple-element.130), channel_id=1, source_target_pairs={{0,1},{1,2},{2,3},{3,4},{4,5},{5,6},{6,7},{7,8},{8,9},{9,10},{10,1... | collective-permute-start | bytes 1179656 | tf_op jit(solution)/shard_map/ppermute | solution.py:32
  151.7 15.6 %collective-permute-start.4 = (bf16[3,1,512,128]{3,2,0,1:T(8,128)(2,1)S(1)}, bf16[3,1,512,128]{3,2,0,1:T(8,128)(2,1)}, u32[]{:S(2)}, u32[]{:S(2)}) collective-permute-start(bf16[3,1,512,128]{3,2,0,1:T(8,128)(2,1)S(1)} %get-tuple-element.129), channel_id=1, source_target_pairs={{1,0},{2,1},{3,2},{4,3},{5,4},{6,5},{7,6},{8,7},{9,8},{10,9},{11,1... | collective-permute-start | bytes 1179656 | tf_op jit(solution)/shard_map/ppermute | solution.py:32
  168.6 6.9 %collective-permute-start.7 = (bf16[1,512,128]{2,1,0:T(8,128)(2,1)S(1)}, bf16[1,512,128]{2,1,0:T(8,128)(2,1)S(1)}, u32[]{:S(2)}, u32[]{:S(2)}) collective-permute-start(bf16[1,512,128]{2,1,0:T(8,128)(2,1)S(1)} %slice_bitcast_fusion.4), channel_id=1, source_target_pairs={{0,16},{16,32},{32,48},{48,64},{64,80},{80,96},{96,112},{112,128},... | collective-permute-start | bytes 393224 | tf_op jit(solution)/shard_map/ppermute | solution.py:32
  172.7 6.7 %collective-permute-start.6 = (bf16[1,512,128]{2,1,0:T(8,128)(2,1)S(1)}, bf16[1,512,128]{2,1,0:T(8,128)(2,1)S(1)}, u32[]{:S(2)}, u32[]{:S(2)}) collective-permute-start(bf16[1,512,128]{2,1,0:T(8,128)(2,1)S(1)} %slice_bitcast_fusion.5), channel_id=1, source_target_pairs={{16,0},{32,16},{48,32},{64,48},{80,64},{96,80},{112,96},{128,112},... | collective-permute-start | bytes 393224 | tf_op jit(solution)/shard_map/ppermute | solution.py:32
  (14 other events, 456.2 us)
Sparse Core Ops, SparseCore 0:
  154.5 284.7 all-reduce.3
where the time goes:
time: 452 us; the launch traced here: 450 us
  waiting for transfers between devices  276 us (61%)
  between operations  66 us (15%)
  other arithmetic  47.2 us (10%)
  starting transfers between devices  27.6 us (6%)
  matrix products  18.7 us (4%)
  local copies, waits for them, and re-layouts  14.7 us (3%)
    psum x1, waiting for transfers between devices, local(): grad_sub, grad_down = lax.psum((grad_sub, grad_down), ('gx', 'gy'))  259 us
    select_n x1, other arithmetic, scatter_back(): pool_grads.at[targets.reshape(-1)].add(beside_all.reshape(-1, C1))  17.2 us
    ppermute x4, waiting for transfers between devices, shifted(): lax.ppermute(value, axis, [(source, source + steps) for source in range(f...  16.9 us
    conv_general_dilated x2, matrix products, convolve(): lax.conv_general_dilated(padded_field, kernel, (1, 1, 1), 'VALID', dimens...  10.3 us
    ppermute x2, starting transfers between devices, padded(): lax.ppermute(lax.slice_in_dim(block, 0, width, axis=dim), axis, backward)  10.1 us
    ppermute x4, starting transfers between devices, shifted(): lax.ppermute(value, axis, [(source, source + steps) for source in range(f...  9.31 us
  transfers between devices with their start and end apart: 9, of which 3 were waited for; matrix products, arithmetic and copies ran while one was open for 7% of the time, Pallas kernels for 0%

commit v1 on v0

v1 whole, which is shorter than its diff:
```python
import math

import jax
import jax.numpy as jnp
from jax import lax
from jax.experimental import pallas as pl
from jax.experimental.pallas import tpu as pltpu
from jax.sharding import PartitionSpec as P

MESH = pl.DeviceIdType.MESH
C1 = 128
C2 = 256
V = 512
X_LO, X_HI, RING = 2, 2, 8
NX = X_LO * X_HI

TILES = 344
HALF = TILES // 2
PART1 = 88
PART2 = HALF - PART1
T1 = PART1 // RING
T1S = -(-T1 // RING)
T2 = PART2 // NX
T2S = -(-T2 // RING)

FACES = ((1, 0), (-1, 0), (0, 1), (0, -1))
EDGES = ((1, 1), (1, -1), (-1, 1), (-1, -1))

F32 = jnp.float32
BF16 = jnp.bfloat16


def field_slabs(source, minus, zero, plus):
    place = lax.broadcasted_iota(jnp.int32, (1, 8, C1), 1)
    below = jnp.where(place == 0, minus, zero)
    above = jnp.where(place == 7, plus, zero)
    return (
        pltpu.roll(source, 1, axis=1) * below,
        source * zero,
        pltpu.roll(source, 7, axis=1) * above,
    )


def kernel(
    near_ref, feat_ref, occ_ref, wsub_ref, wdown_ref, cot_ref,
    out_ref, gfeat_ref, gsum_ref,
    mask_ref, shuf_ref, field_ref, cols_ref, wflip_ref, kids_ref,
    sface, sedge, rface, redge,
    g32, g16, rc, s16, r1a, r1b, q1, q2, r2a, r2b, e1, e2, f1, f2,
    hs_sem, hr_sem, c_sem, a1_sem, b1_sem, a2_sem, b2_sem, a3_sem, b3_sem,
    a4_sem, b4_sem, a5_sem, b5_sem, a6_sem, b6_sem,
):
    gx, gy = lax.axis_index("gx"), lax.axis_index("gy")
    core = gx % 2
    y = (gx // 2) % RING
    x = (gy % X_HI) * X_LO + gx // (2 * RING)
    z = gy // X_HI

    def device(px, py, pz, pc):
        return ((px % X_LO) * (2 * RING) + py * 2 + pc, pz * X_HI + px // X_LO)

    pa = jnp.where(core == 0, y, z)
    pb = jnp.where(core == 0, z, y)

    def on_a(p):
        return device(x, jnp.where(core == 0, p, y), jnp.where(core == 0, z, p), core)

    def on_b(p):
        return device(x, jnp.where(core == 0, y, p), jnp.where(core == 0, p, z), core)

    def on_x(p):
        return device(p, y, z, core)

    partner = device(x, y, z, 1 - core)
    tiles_x, tiles_y = 2 * RING * X_LO, RING * X_HI

    def tile_at(dx, dy):
        return ((gx + dx + tiles_x) % tiles_x, (gy + dy + tiles_y) % tiles_y)

    barrier = pltpu.get_barrier_semaphore()

    def greet(target):
        pl.semaphore_signal(barrier, inc=1, device_id=target, device_id_type=MESH)

    for dx, dy in FACES + EDGES:
        greet(tile_at(dx, dy))
    greet(partner)

    def greet_rings(s, carry):
        greet(on_a((pa + s) % RING))
        greet(on_b((pb + s) % RING))
        return carry

    lax.fori_loop(1, RING, greet_rings, 0)

    def greet_x(s, carry):
        greet(on_x((x + s) % NX))
        return carry

    lax.fori_loop(1, NX, greet_x, 0)

    def remote(src, dst, send, recv, target):
        return pltpu.make_async_remote_copy(
            src_ref=src, dst_ref=dst, send_sem=send, recv_sem=recv,
            device_id=target, device_id_type=MESH,
        )

    def halo_copies(which):
        copies = []
        for d, (dx, dy) in enumerate(FACES):
            copies.append(
                remote(sface.at[which, d], rface.at[which, d], hs_sem.at[which, d],
                       hr_sem.at[which, d], tile_at(dx, dy))
            )
        for d, (dx, dy) in enumerate(EDGES):
            copies.append(
                remote(sedge.at[which, d], redge.at[which, d], hs_sem.at[which, 4 + d],
                       hr_sem.at[which, 4 + d], tile_at(dx, dy))
            )
        return copies

    def stage_halo(which, value):
        cells = value.reshape(8, 8, 8, C1)
        side = {1: 7, -1: 0}
        for d, (dx, dy) in enumerate(FACES):
            face = cells[side[dx]] if dx else cells[:, side[dy]]
            sface[which, d] = face.reshape(64, C1).astype(BF16)
        for d, (dx, dy) in enumerate(EDGES):
            edge = cells[side[dx], side[dy]]
            sedge[which, d] = jnp.concatenate([edge, edge], axis=0).astype(BF16)

    def named(dx, dy, d0, d1):
        return [
            jnp.where(near_ref[0, 9 * (d0 + 1) + 3 * (d1 + 1) + l] == 3 * (dx + 1) + dy + 1, 1.0, 0.0)
            for l in range(3)
        ]

    def columns(which, value):
        zero, one = F32(0.0), F32(1.0)
        center = field_slabs(value.reshape(64, 8, C1), zero, one, zero)
        for l in range(3):
            field_ref[l, 1:9, 1:9] = center[l].reshape(8, 8, 8, C1)
        corner = {}

        def add_corner(cx, cy, slabs):
            for l in range(3):
                old = corner.get((cx, cy, l))
                corner[cx, cy, l] = slabs[l] if old is None else old + slabs[l]

        place = {1: 9, -1: 0}
        near_row = {1: 0, -1: 7}
        for dx, dy in FACES:
            slot = FACES.index((-dx, -dy))
            face = rface[which, slot].astype(F32).reshape(8, 8, C1)
            slabs = field_slabs(face, *named(dx, dy, dx, dy))
            for l in range(3):
                if dx:
                    field_ref[l, place[dx], 1:9] = slabs[l]
                else:
                    for r in range(8):
                        field_ref[l, 1 + r, place[dy]] = slabs[l][r]
            for side in (1, -1):
                row = near_row[side]
                d0, d1 = (dx, side) if dx else (side, dy)
                add_corner(
                    place[d0], place[d1],
                    field_slabs(face[row : row + 1], *named(dx, dy, d0, d1)),
                )
        for dx, dy in EDGES:
            slot = EDGES.index((-dx, -dy))
            edge = redge[which, slot].astype(F32)[0:8].reshape(1, 8, C1)
            add_corner(place[dx], place[dy], field_slabs(edge, *named(dx, dy, dx, dy)))
        for (cx, cy, l), slab in corner.items():
            field_ref[l, cx, cy] = slab[0]
        for i in range(3):
            for j in range(3):
                for l in range(3):
                    k = 9 * i + 3 * j + l
                    window = field_ref[l, i : i + 8, j : j + 8]
                    cols_ref[:, k * C1 : (k + 1) * C1] = window.reshape(V, C1).astype(BF16)

    def split_children(value):
        cells = value.reshape(8, 4, 2, 8, C1)
        for ey in range(2):
            shuf_ref[ey * 256 : (ey + 1) * 256] = cells[:, :, ey].reshape(256, C1)
        children = [None] * 8
        for ey in range(2):
            for ez in range(2):
                half = shuf_ref[pl.ds(ey * 256 + ez, 128, stride=2), :].reshape(4, 2, 16, C1)
                for ex in range(2):
                    children[4 * ex + 2 * ey + ez] = half[:, ex].reshape(64, C1)
        return children

    def join_children(children):
        for ey in range(2):
            for ez in range(2):
                pair = [children[4 * ex + 2 * ey + ez].reshape(4, 1, 16, C1) for ex in range(2)]
                shuf_ref[pl.ds(ey * 256 + ez, 128, stride=2), :] = jnp.concatenate(
                    pair, axis=1
                ).reshape(128, C1)
        sides = [shuf_ref[e * 256 : (e + 1) * 256].reshape(8, 4, 1, 8, C1) for e in range(2)]
        return jnp.concatenate(sides, axis=2).reshape(V, C1)

    for r in range(4):
        line = occ_ref[0:1, r * 128 : (r + 1) * 128].astype(F32)
        mask_ref[r * 128 : (r + 1) * 128] = jnp.broadcast_to(line, (128, 128)).T
    masked = feat_ref[...].astype(F32) * mask_ref[...]
    stage_halo(0, masked)
    pl.semaphore_wait(barrier, 9 + 2 * (RING - 1) + NX - 1)
    halo = halo_copies(0)
    for copy in halo:
        copy.start()

    for k in range(27):
        wflip_ref[:, k * C1 : (k + 1) * C1] = wsub_ref[(26 - k) * C1 : (27 - k) * C1]
    coarse = None
    for child in split_children(mask_ref[...]):
        coarse = child if coarse is None else jnp.maximum(coarse, child)
    coarse = jnp.concatenate([coarse, coarse], axis=1)
    seeded = (cot_ref[...].astype(F32) * coarse).astype(BF16)
    spread = lax.dot_general(
        seeded, wdown_ref[...], (((1,), (1,)), ((), ())), preferred_element_type=F32
    )
    hidden_grad = join_children([spread[:, r * C1 : (r + 1) * C1] for r in range(8)])

    for copy in halo:
        copy.wait_recv()
    columns(0, masked)
    preact = jnp.dot(cols_ref[...], wsub_ref[...], preferred_element_type=F32)
    sig = jax.nn.sigmoid(preact)
    mask = mask_ref[...]
    hidden = (preact * sig * mask).astype(BF16).astype(F32)
    pre_grad = (hidden_grad * (sig * (1.0 + preact * (1.0 - sig))) * mask).astype(BF16).astype(F32)
    stage_halo(1, pre_grad)
    halo2 = halo_copies(1)
    for copy in halo2:
        copy.start()

    for r, child in enumerate(split_children(hidden)):
        kids_ref[:, r * C1 : (r + 1) * C1] = child.astype(BF16)

    def put(tile, value):
        count = value.shape[0] // 16
        value = value.reshape(count, 16, C1)
        g32[tile : tile + count] = value
        g16[tile : tile + count] = value.astype(BF16)

    grad_down = lax.dot_general(
        kids_ref[...], seeded, (((0,), (0,)), ((), ())), preferred_element_type=F32
    )
    put(216, grad_down[:, :C1])
    put(280, grad_down[:, C1:])
    turned = pre_grad.T.astype(BF16)
    for k in range(27):
        block = jnp.dot(
            turned, cols_ref[:, k * C1 : (k + 1) * C1], preferred_element_type=F32
        )
        put(8 * k, block.T)

    mine, theirs = core * HALF, (1 - core) * HALF
    starts = (0, PART1)
    sizes = (PART1, PART2)
    core_copies = [
        remote(g16.at[pl.ds(theirs + starts[p], sizes[p])], rc.at[pl.ds(starts[p], sizes[p])],
               c_sem.at[0, p], c_sem.at[1, p], partner)
        for p in range(2)
    ]
    for copy in core_copies:
        copy.start()

    def ring_copy(s, n, place, where, src, dst, sem):
        return remote(src, dst, sem.at[0, s], sem.at[1, s], where((place + s) % n))

    def start_all(n, make):
        def body(s, carry):
            make(s).start()
            return carry

        lax.fori_loop(1, n, body, 0)

    def recv_all(n, make):
        def body(s, carry):
            make(s).wait_recv()
            return carry

        lax.fori_loop(1, n, body, 0)

    def send_all(n, make):
        def body(s, carry):
            make(s).wait_send()
            return carry

        lax.fori_loop(1, n, body, 0)

    def scatter1a(s):
        return ring_copy(s, RING, pa, on_a, s16.at[pl.ds(((pa + s) % RING) * T1, T1)], r1a.at[s], a1_sem)

    def scatter1b(s):
        return ring_copy(s, NX, x, on_x, s16.at[pl.ds(PART1 + ((x + s) % NX) * T2, T2)], r1b.at[s], b1_sem)

    def scatter2a(s):
        return ring_copy(s, RING, pb, on_b, q1.at[pl.ds(((pb + s) % RING) * T1S, T1S)], r2a.at[s], a2_sem)

    def scatter2b(s):
        return ring_copy(s, RING, pa, on_a, q2.at[pl.ds(((pa + s) % RING) * T2S, T2S)], r2b.at[s], b2_sem)

    def swap3a(s):
        return ring_copy(s, NX, x, on_x, e1.at[x], e1.at[x], a3_sem)

    def swap3b(s):
        return ring_copy(s, RING, pb, on_b, e2.at[pb], e2.at[pb], b3_sem)

    def gather2a(s):
        own = f1.at[pl.ds(pb * T1S, T1S)]
        return ring_copy(s, RING, pb, on_b, own, own, a4_sem)

    def gather2b(s):
        own = f2.at[pl.ds(pa * T2S, T2S)]
        return ring_copy(s, RING, pa, on_a, own, own, b4_sem)

    def piece1(p):
        return gsum_ref.at[pl.ds(mine + p * T1, T1)]

    def piece2(p):
        return gsum_ref.at[pl.ds(mine + PART1 + p * T2, T2)]

    def gather1a(s):
        return ring_copy(s, RING, pa, on_a, piece1(pa), piece1(pa), a5_sem)

    def gather1b(s):
        return ring_copy(s, NX, x, on_x, piece2(x), piece2(x), b5_sem)

    def across_a(s):
        piece = piece1((pa - s + RING) % RING)
        return remote(piece, piece, a6_sem.at[0, s], a6_sem.at[1, s], partner)

    def across_b(s):
        piece = piece2((x - s + NX) % NX)
        return remote(piece, piece, b6_sem.at[0, s], b6_sem.at[1, s], partner)

    def pair_sum(at, count):
        return g32[pl.ds(mine + at, count)] + rc[pl.ds(at, count)].astype(F32)

    core_copies[0].wait_recv()
    s16[0:PART1] = pair_sum(0, PART1).astype(BF16)
    start_all(RING, scatter1a)
    core_copies[1].wait_recv()
    s16[PART1:HALF] = pair_sum(PART1, PART2).astype(BF16)
    start_all(NX, scatter1b)

    for copy in halo2:
        copy.wait_recv()
    columns(1, pre_grad)
    gfeat = lax.dot_general(
        cols_ref[...], wflip_ref[...], (((1,), (1,)), ((), ())), preferred_element_type=F32
    )
    gfeat_ref[...] = (gfeat * mask_ref[...]).astype(BF16)
    output = jnp.dot(kids_ref[...], wdown_ref[...], preferred_element_type=F32)
    out_ref[...] = (output * coarse).astype(BF16)

    recv_all(RING, scatter1a)
    total = pair_sum(pa * T1, T1)
    for s in range(1, RING):
        total = total + r1a[s].astype(F32)
    q1[0:T1] = total.astype(BF16)
    if T1S * RING > T1:
        q1[T1 : T1S * RING] = jnp.zeros((T1S * RING - T1, 16, C1), BF16)
    start_all(RING, scatter2a)

    recv_all(NX, scatter1b)
    total = pair_sum(PART1 + x * T2, T2)
    for s in range(1, NX):
        total = total + r1b[s].astype(F32)
    q2[0:T2] = total.astype(BF16)
    if T2S * RING > T2:
        q2[T2 : T2S * RING] = jnp.zeros((T2S * RING - T2, 16, C1), BF16)
    start_all(RING, scatter2b)

    recv_all(RING, scatter2a)
    total = q1[pl.ds(pb * T1S, T1S)].astype(F32)
    for s in range(1, RING):
        total = total + r2a[s].astype(F32)
    e1[x] = total.astype(BF16)
    start_all(NX, swap3a)

    recv_all(RING, scatter2b)
    total = q2[pl.ds(pa * T2S, T2S)].astype(F32)
    for s in range(1, RING):
        total = total + r2b[s].astype(F32)
    e2[pb] = total.astype(BF16)
    start_all(RING, swap3b)

    recv_all(NX, swap3a)
    total = e1[0].astype(F32)
    for p in range(1, NX):
        total = total + e1[p].astype(F32)
    f1[pl.ds(pb * T1S, T1S)] = total.astype(BF16)
    start_all(RING, gather2a)

    recv_all(RING, swap3b)
    total = e2[0].astype(F32)
    for p in range(1, RING):
        total = total + e2[p].astype(F32)
    f2[pl.ds(pa * T2S, T2S)] = total.astype(BF16)
    start_all(RING, gather2b)

    recv_all(RING, gather2a)
    gsum_ref[pl.ds(mine + pa * T1, T1)] = f1[0:T1]
    start_all(RING, gather1a)
    across_a(0).start()

    recv_all(RING, gather2b)
    gsum_ref[pl.ds(mine + PART1 + x * T2, T2)] = f2[0:T2]
    start_all(NX, gather1b)
    across_b(0).start()

    def pass_a(s, carry):
        gather1a(s).wait_recv()
        across_a(s).start()
        return carry

    def pass_b(s, carry):
        gather1b(s).wait_recv()
        across_b(s).start()
        return carry

    lax.fori_loop(1, NX, pass_b, 0)
    lax.fori_loop(1, RING, pass_a, 0)
    across_b(0).wait_recv()
    recv_all(NX, across_b)
    across_a(0).wait_recv()
    recv_all(RING, across_a)

    for copy in halo + halo2 + core_copies:
        copy.wait_send()
    for make in (scatter1a, scatter2a, scatter2b, swap3b, gather2a, gather2b, gather1a, across_a):
        send_all(RING, make)
    for make in (scatter1b, swap3a, gather1b, across_b):
        send_all(NX, make)
    across_a(0).wait_send()
    across_b(0).wait_send()


def local(features, occupancy, neighbours, weight_sub, weight_down, cotangent):
    def tiles(*shape):
        return pltpu.VMEM(shape + (16, C1), BF16)

    vmem = pl.BlockSpec(memory_space=pltpu.VMEM)
    ring, short = pltpu.SemaphoreType.DMA((2, RING)), pltpu.SemaphoreType.DMA((2, NX))
    output, grad_features, sums = pl.pallas_call(
        kernel,
        out_shape=(
            jax.ShapeDtypeStruct((64, C2), BF16),
            jax.ShapeDtypeStruct((V, C1), BF16),
            jax.ShapeDtypeStruct((TILES, 16, C1), BF16),
        ),
        in_specs=[pl.BlockSpec(memory_space=pltpu.SMEM)] + [vmem] * 5,
        out_specs=(vmem, vmem, vmem),
        scratch_shapes=[
            pltpu.VMEM((V, C1), F32),
            pltpu.VMEM((V, C1), F32),
            pltpu.VMEM((3, 10, 10, 8, C1), F32),
            pltpu.VMEM((V, 27 * C1), BF16),
            pltpu.VMEM((C1, 27 * C1), BF16),
            pltpu.VMEM((64, 8 * C1), BF16),
            pltpu.VMEM((2, 4, 64, C1), BF16),
            pltpu.VMEM((2, 4, 16, C1), BF16),
            pltpu.VMEM((2, 4, 64, C1), BF16),
            pltpu.VMEM((2, 4, 16, C1), BF16),
            pltpu.VMEM((TILES, 16, C1), F32),
            tiles(TILES), tiles(HALF), tiles(HALF),
            tiles(RING, T1), tiles(NX, T2),
            tiles(T1S * RING), tiles(T2S * RING),
            tiles(RING, T1S), tiles(RING, T2S),
            tiles(NX, T1S), tiles(RING, T2S),
            tiles(T1S * RING), tiles(T2S * RING),
            pltpu.SemaphoreType.DMA((2, 8)), pltpu.SemaphoreType.DMA((2, 8)),
            pltpu.SemaphoreType.DMA((2, 2)),
            ring, short, ring, ring, short, ring, ring, ring, ring, short, ring, short,
        ],
        compiler_params=pltpu.CompilerParams(
            collective_id=0, has_side_effects=True, vmem_limit_bytes=48 * 1024 * 1024
        ),
    )(
        neighbours.reshape(1, 27),
        features.reshape(V, C1),
        occupancy.reshape(1, V),
        weight_sub.reshape(27 * C1, C1),
        weight_down.reshape(8 * C1, C2),
        cotangent.reshape(64, C2),
    )
    scale = 1.0 / math.sqrt(lax.axis_size("gx") * lax.axis_size("gy") * V)
    grad_sub = sums[:216].reshape(27, C1, C1).astype(F32) * scale
    grad_down = sums[216:].reshape(2, 8, C1, C1).astype(F32) * scale
    return (
        output.reshape(1, 1, 1, 64, C2),
        grad_features.reshape(1, 1, 1, V, C1),
        grad_sub,
        jnp.concatenate([grad_down[0], grad_down[1]], axis=2),
    )


def solution(mesh):
    return jax.shard_map(
        local,
        mesh=mesh,
        in_specs=(
            P("gx", "gy", None, None, None),
            P("gx", "gy", None, None),
            P("gx", "gy", None, None),
            P(),
            P(),
            P("gx", "gy", None, None, None),
        ),
        out_specs=(P("gx", "gy", None, None, None), P("gx", "gy", None, None, None), P(), P()),
        check_vma=False,
    )
```

time: 452 us -> 68.9 us (0.15)
  waiting for transfers between devices: 276 us -> 0 us
  between operations: 66 us -> 0.67 us
  Pallas kernels: 0 us -> 58.9 us
  other arithmetic: 47.2 us -> 2.44 us
  starting transfers between devices: 27.6 us -> 0 us
  matrix products: 18.7 us -> 0 us
  local copies, waits for them, and re-layouts: 14.7 us -> 6.54 us
    psum x1 -> x0, waiting for transfers between devices: 259 us -> none  [local(): grad_sub, grad_down = lax.psum((grad_sub, grad_down), ('gx', 'gy'))]
    pallas_call x0 -> x1, Pallas kernels: none -> 58.9 us  [local(): pl.pallas_call(kernel, out_shape=(jax.ShapeDtypeStruct((64, C2), BF16), j...]
    ppermute x8 -> x0, starting transfers between devices: 27.5 us -> none  [the longest x2 10.1 us: padded(): lax.ppermute(lax.slice_in_dim(block, 0, width, axis=dim), axis, backward)]
    select_n x15 -> x0, other arithmetic: 18.2 us -> none  [the longest x1 17.2 us: scatter_back(): pool_grads.at[targets.reshape(-1)].add(beside_all.reshape(-1, C1))]
    ppermute x8 -> x0, waiting for transfers between devices: 16.9 us -> none  [the longest x4 16.9 us: shifted(): lax.ppermute(value, axis, [(source, source + steps) for source in range(f...]
    conv_general_dilated x2 -> x0, matrix products: 10.3 us -> none  [convolve(): lax.conv_general_dilated(padded_field, kernel, (1, 1, 1), 'VALID', dimens...]
    concatenate x3 -> x1, other arithmetic: 10.3 us -> 1.04 us  [local(): jnp.concatenate([grad_down[0], grad_down[1]], axis=2)]
    scatter-add x1 -> x0, other arithmetic: 7.84 us -> none  [scatter_back(): pool_grads.at[targets.reshape(-1)].add(beside_all.reshape(-1, C1))]
  transfers between devices with their start and end apart: 9 -> 0, of which waited for: 3 -> 0; matrix products, arithmetic and copies ran while one was open for 7% -> 0% of each run, Pallas kernels for 0% -> 0%
where the time goes in v1:
time: 68.9 us; the launch traced here: 68.5 us
  Pallas kernels  58.9 us (85%)
  local copies, waits for them, and re-layouts  6.54 us (9%)
  other arithmetic  2.44 us (4%)
    pallas_call x1, Pallas kernels, local(): pl.pallas_call(kernel, out_shape=(jax.ShapeDtypeStruct((64, C2), BF16), j...  58.9 us
    unnamed x14, local copies, waits for them, and re-layouts  6.47 us

profile of v1, /device:TPU:1, one launch (start us, length us, event | category | flops | bytes accessed | tf_op | source)
XLA Modules:
  0.0 68.5 jit_solution(16885473990031459419)
XLA Ops:
  0.6 0.0 copy-start
  0.6 1.2 %copy-done = bf16[27,128,128]{2,1,0:T(8,128)(2,1)S(1)} copy-done((bf16[27,128,128]{2,1,0:T(8,128)(2,1)S(1)}, bf16[27,128,128]{2,1,0:T(8,128)(2,1)}, u32[]{:S(2)}) %copy-start) | copy-done | bytes 884760
  1.8 0.0 copy-start.1
  1.8 1.0 %copy-done.1 = bf16[8,128,256]{2,1,0:T(8,128)(2,1)S(1)} copy-done((bf16[8,128,256]{2,1,0:T(8,128)(2,1)S(1)}, bf16[8,128,256]{2,1,0:T(8,128)(2,1)}, u32[]{:S(2)}) %copy-start.1) | copy-done | bytes 524312
  2.8 0.0 copy-start.2
  2.8 0.9 %copy-done.2 = bf16[1,1,1,512,128]{4,3,2,1,0:T(8,128)(2,1)S(1)} copy-done((bf16[1,1,1,512,128]{4,3,2,1,0:T(8,128)(2,1)S(1)}, bf16[1,1,1,512,128]{4,3,2,1,0:T(8,128)(2,1)}, u32[]{:S(2)}) %copy-start.2) | copy-done | bytes 131096
  3.7 0.0 copy-start.3
  3.8 0.8 %copy-done.3 = bf16[1,1,1,64,256]{4,3,2,1,0:T(8,128)(2,1)S(1)} copy-done((bf16[1,1,1,64,256]{4,3,2,1,0:T(8,128)(2,1)S(1)}, bf16[1,1,1,64,256]{4,3,2,1,0:T(8,128)(2,1)}, u32[]{:S(2)}) %copy-start.3) | copy-done | bytes 32792
  4.5 0.0 copy-start.4
  4.5 0.7 copy-done.4
  5.2 0.0 copy-start.5
  5.2 0.7 copy-done.5
  5.8 58.9 %shard_map.93 = (bf16[64,256]{1,0:T(8,128)(2,1)S(1)}, bf16[512,128]{1,0:T(8,128)(2,1)S(1)}, bf16[344,16,128]{2,1,0:T(8,128)(2,1)S(1)}) custom-call(s32[1,27]{1,0:T(1,128)S(1)} %bitcast.18, bf16[512,128]{1,0:T(8,128)(2,1)S(1)} %bitcast.13, s32[1,512]{1,0:T(1,128)S(1)} %bitcast.17, bf16[3456,128]{1,0:T(8,128)(2,1)S(1)} %bitcast.11, ...), custom_call_target="tpu_custom_call" | custom-call | tf_op jit(solution)/shard_map/pallas_call | solution.py:450
  64.7 0.1 convert_multiply_fusion.1
  64.8 0.1 fusion
  64.9 1.0 %pad_maximum_fusion = f32[8,128,256]{2,1,0:T(8,128)} fusion(f32[8,128,128]{2,1,0:T(8,128)S(1)} %bitcast.20, f32[8,128,128]{2,1,0:T(8,128)S(1)} %bitcast.19), kind=kLoop, calls=%fused_computation.1 | loop fusion | flops 262144 | bytes 2097152 | tf_op jit(solution)/shard_map/concatenate | solution.py:499
  65.9 1.3 %convert_multiply_fusion = f32[216,16,128]{2,1,0:T(8,128)} fusion(bf16[344,16,128]{2,1,0:T(8,128)(2,1)S(1)} %get-tuple-element.9), kind=kLoop, calls=%fused_computation | loop fusion | flops 884736 | bytes 2654208 | tf_op jit(solution)/shard_map/mul | solution.py:493
  67.3 0.6 copy.12
  67.9 0.7 copy.13
Async XLA Ops:
  0.6 1.2 %copy-start = (bf16[27,128,128]{2,1,0:T(8,128)(2,1)S(1)}, bf16[27,128,128]{2,1,0:T(8,128)(2,1)}, u32[]{:S(2)}) copy-start(bf16[27,128,128]{2,1,0:T(8,128)(2,1)} %param.9) | copy-start | bytes 2654212
  1.8 1.0 %copy-start.1 = (bf16[8,128,256]{2,1,0:T(8,128)(2,1)S(1)}, bf16[8,128,256]{2,1,0:T(8,128)(2,1)}, u32[]{:S(2)}) copy-start(bf16[8,128,256]{2,1,0:T(8,128)(2,1)} %param.10) | copy-start | bytes 1572868
  2.8 0.9 %copy-start.2 = (bf16[1,1,1,512,128]{4,3,2,1,0:T(8,128)(2,1)S(1)}, bf16[1,1,1,512,128]{4,3,2,1,0:T(8,128)(2,1)}, u32[]{:S(2)}) copy-start(bf16[1,1,1,512,128]{4,3,2,1,0:T(8,128)(2,1)} %param.6) | copy-start | bytes 393220
  3.7 0.8 %copy-start.3 = (bf16[1,1,1,64,256]{4,3,2,1,0:T(8,128)(2,1)S(1)}, bf16[1,1,1,64,256]{4,3,2,1,0:T(8,128)(2,1)}, u32[]{:S(2)}) copy-start(bf16[1,1,1,64,256]{4,3,2,1,0:T(8,128)(2,1)} %param.11) | copy-start | bytes 98308
  4.5 0.7 copy-start.4
  5.2 0.7 copy-start.5

commit v2 on v1

v2 whole, which is shorter than its diff:
```python
import functools
import math

import jax
import jax.numpy as jnp
from jax import lax
from jax.experimental import pallas as pl
from jax.experimental.pallas import tpu as pltpu
from jax.sharding import PartitionSpec as P

MESH = pl.DeviceIdType.MESH
C1 = 128
C2 = 256
V = 512
X_LO, X_HI, RING = 2, 2, 8
NX = X_LO * X_HI

SUB_OWNERS = RING - 1
SUB_T = -(-108 // (NX * SUB_OWNERS))
SUB = NX * SUB_OWNERS * SUB_T
HALF = SUB + 64
ORDER = (2, 1, 3, 0) if NX == 4 else (1, 0)
PARTS = ((SUB, RING, 64 // (NX * RING)), (0, SUB_OWNERS, SUB_T))


FACES = ((1, 0), (-1, 0), (0, 1), (0, -1))
EDGES = ((1, 1), (1, -1), (-1, 1), (-1, -1))

F32 = jnp.float32
BF16 = jnp.bfloat16


def field_slabs(source, minus, zero, plus):
    place = lax.broadcasted_iota(jnp.int32, (1, 8, C1), 1)
    below = jnp.where(place == 0, minus, zero)
    above = jnp.where(place == 7, plus, zero)
    return (
        pltpu.roll(source, 1, axis=1) * below,
        source * zero,
        pltpu.roll(source, 7, axis=1) * above,
    )


def kernel(
    near_in, feat_in, occ_in, wsub_in, wdown_in, cot_in,
    out_ref, gfeat_ref, gsum_ref,
    near_ref, feat_ref, occ_ref, wsub_ref, wdown_ref, cot_ref,
    mask_ref, shuf_ref, field_ref, cols_ref, wflip_ref, kids_ref,
    shalo, rhalo, g32, g16, in_sem, hs_sem, hr_sem, *part_refs,
):
    loads = [
        pltpu.make_async_copy(src, dst, in_sem.at[i])
        for i, (src, dst) in enumerate(
            (
                (occ_in, occ_ref), (feat_in, feat_ref), (near_in, near_ref),
                (wdown_in, wdown_ref), (cot_in, cot_ref), (wsub_in, wsub_ref),
            )
        )
    ]
    for load in loads:
        load.start()
    gx, gy = lax.axis_index("gx"), lax.axis_index("gy")
    core = gx % 2
    y = (gx // 2) % RING
    x = (gy % X_HI) * X_LO + gx // (2 * RING)
    z = gy // X_HI

    def device(px, py, pz, pc):
        return ((px % X_LO) * (2 * RING) + py * 2 + pc, pz * X_HI + px // X_LO)

    pa = jnp.where(core == 0, y, z)
    pb = jnp.where(core == 0, z, y)

    def on_plane(px, p):
        return device(px, jnp.where(core == 0, p, y), jnp.where(core == 0, z, p), core)

    def on_b(p):
        return device(x, jnp.where(core == 0, y, p), jnp.where(core == 0, p, z), core)

    partner = device(x, y, z, 1 - core)
    tiles_x, tiles_y = 2 * RING * X_LO, RING * X_HI

    def tile_at(dx, dy):
        return ((gx + dx + tiles_x) % tiles_x, (gy + dy + tiles_y) % tiles_y)

    barrier = pltpu.get_barrier_semaphore()

    def greet(target):
        pl.semaphore_signal(barrier, inc=1, device_id=target, device_id_type=MESH)

    for dx, dy in FACES + EDGES:
        greet(tile_at(dx, dy))
    greet(partner)

    def greet_plane(i, carry):
        greet(on_plane((x + i // RING) % NX, (pa + i) % RING))
        return carry

    lax.fori_loop(1, NX * RING, greet_plane, 0)

    def greet_ring(s, carry):
        greet(on_b((pb + s) % RING))
        return carry

    lax.fori_loop(1, RING, greet_ring, 0)

    def remote(src, dst, send, recv, target):
        return pltpu.make_async_remote_copy(
            src_ref=src, dst_ref=dst, send_sem=send, recv_sem=recv,
            device_id=target, device_id_type=MESH,
        )

    def send_halo(which):
        for d, (dx, dy) in enumerate(FACES):
            region = pl.ds(4 * d, 4)
            remote(shalo.at[which, region], rhalo.at[which, region], hs_sem.at[which],
                   hr_sem.at[which], tile_at(dx, dy)).start()
        for d, (dx, dy) in enumerate(EDGES):
            region = pl.ds(16 + d, 1)
            remote(shalo.at[which, region], rhalo.at[which, region], hs_sem.at[which],
                   hr_sem.at[which], tile_at(dx, dy)).start()

    def whole_halo(which):
        return remote(shalo.at[which], rhalo.at[which], hs_sem.at[which], hr_sem.at[which], partner)

    def stage_halo(which, value):
        cells = value.reshape(8, 8, 8, C1)
        side = {1: 7, -1: 0}
        for d, (dx, dy) in enumerate(FACES):
            face = cells[side[dx]] if dx else cells[:, side[dy]]
            shalo[which, 4 * d : 4 * d + 4] = face.reshape(4, 16, C1).astype(BF16)
        for d, (dx, dy) in enumerate(EDGES):
            edge = cells[side[dx], side[dy]]
            shalo[which, 16 + d] = jnp.concatenate([edge, edge], axis=0).astype(BF16)

    def named(dx, dy, d0, d1):
        return [
            jnp.where(near_ref[0, 9 * (d0 + 1) + 3 * (d1 + 1) + l] == 3 * (dx + 1) + dy + 1, 1.0, 0.0)
            for l in range(3)
        ]

    def center(value):
        slabs = field_slabs(value.reshape(64, 8, C1), F32(0.0), F32(1.0), F32(0.0))
        for l in range(3):
            field_ref[l, 1:9, 1:9] = slabs[l].reshape(8, 8, 8, C1)

    def columns(which):
        corner = {}

        def add_corner(cx, cy, slabs):
            for l in range(3):
                old = corner.get((cx, cy, l))
                corner[cx, cy, l] = slabs[l] if old is None else old + slabs[l]

        place = {1: 9, -1: 0}
        near_row = {1: 0, -1: 7}
        for dx, dy in FACES:
            slot = FACES.index((-dx, -dy))
            face = rhalo[which, 4 * slot : 4 * slot + 4].astype(F32).reshape(8, 8, C1)
            slabs = field_slabs(face, *named(dx, dy, dx, dy))
            for l in range(3):
                if dx:
                    field_ref[l, place[dx], 1:9] = slabs[l]
                else:
                    for r in range(8):
                        field_ref[l, 1 + r, place[dy]] = slabs[l][r]
            for side in (1, -1):
                row = near_row[side]
                d0, d1 = (dx, side) if dx else (side, dy)
                add_corner(
                    place[d0], place[d1],
                    field_slabs(face[row : row + 1], *named(dx, dy, d0, d1)),
                )
        for dx, dy in EDGES:
            slot = EDGES.index((-dx, -dy))
            edge = rhalo[which, 16 + slot].astype(F32)[0:8].reshape(1, 8, C1)
            add_corner(place[dx], place[dy], field_slabs(edge, *named(dx, dy, dx, dy)))
        for (cx, cy, l), slab in corner.items():
            field_ref[l, cx, cy] = slab[0]
        for i in range(3):
            for j in range(3):
                for l in range(3):
                    k = 9 * i + 3 * j + l
                    window = field_ref[l, i : i + 8, j : j + 8]
                    cols_ref[:, k * C1 : (k + 1) * C1] = window.reshape(V, C1).astype(BF16)

    def split_children(value):
        cells = value.reshape(8, 4, 2, 8, C1)
        for ey in range(2):
            shuf_ref[ey * 256 : (ey + 1) * 256] = cells[:, :, ey].reshape(256, C1)
        children = [None] * 8
        for ey in range(2):
            for ez in range(2):
                half = shuf_ref[pl.ds(ey * 256 + ez, 128, stride=2), :].reshape(4, 2, 16, C1)
                for ex in range(2):
                    children[4 * ex + 2 * ey + ez] = half[:, ex].reshape(64, C1)
        return children

    def join_children(children):
        for ey in range(2):
            for ez in range(2):
                pair = [children[4 * ex + 2 * ey + ez].reshape(4, 1, 16, C1) for ex in range(2)]
                shuf_ref[pl.ds(ey * 256 + ez, 128, stride=2), :] = jnp.concatenate(
                    pair, axis=1
                ).reshape(128, C1)
        sides = [shuf_ref[e * 256 : (e + 1) * 256].reshape(8, 4, 1, 8, C1) for e in range(2)]
        return jnp.concatenate(sides, axis=2).reshape(V, C1)

    loads[0].wait()
    for r in range(4):
        line = occ_ref[0:1, r * 128 : (r + 1) * 128].astype(F32)
        mask_ref[r * 128 : (r + 1) * 128] = jnp.broadcast_to(line, (128, 128)).T
    loads[1].wait()
    masked = feat_ref[...].astype(F32) * mask_ref[...]
    stage_halo(0, masked)
    pl.semaphore_wait(barrier, 9 + NX * RING - 1 + RING - 1)
    send_halo(0)

    center(masked)
    for load in loads[2:]:
        load.wait()
    for k in range(27):
        wflip_ref[:, k * C1 : (k + 1) * C1] = wsub_ref[(26 - k) * C1 : (27 - k) * C1]
    coarse = None
    for child in split_children(mask_ref[...]):
        coarse = child if coarse is None else jnp.maximum(coarse, child)
    coarse = jnp.concatenate([coarse, coarse], axis=1)
    seeded = (cot_ref[...].astype(F32) * coarse).astype(BF16)
    spread = lax.dot_general(
        seeded, wdown_ref[...], (((1,), (1,)), ((), ())), preferred_element_type=F32
    )
    hidden_grad = join_children([spread[:, r * C1 : (r + 1) * C1] for r in range(8)])

    whole_halo(0).wait_recv()
    columns(0)
    preact = jnp.dot(cols_ref[...], wsub_ref[...], preferred_element_type=F32)
    sig = jax.nn.sigmoid(preact)
    mask = mask_ref[...]
    hidden = (preact * sig * mask).astype(BF16).astype(F32)
    for r, child in enumerate(split_children(hidden)):
        kids_ref[:, r * C1 : (r + 1) * C1] = child.astype(BF16)

    mine, theirs = core * HALF, (1 - core) * HALF

    def put(tile, value):
        value = value.reshape(value.shape[0] // 16, 16, C1)
        g32[tile : tile + value.shape[0]] = value
        g16[tile : tile + value.shape[0]] = value.astype(BF16)

    class Part:
        def __init__(self, index):
            self.at, self.owners, self.t = PARTS[index]
            self.group = self.owners * self.t
            self.count = NX * self.group
            (self.rc, self.s16, self.r1, self.e,
             self.send, self.recv, self.late) = part_refs[7 * index : 7 * index + 7]

        def when_owner(self, body):
            if self.owners == RING:
                body()
            else:
                pl.when(pa < self.owners)(body)

        def unless_owner(self, body):
            if self.owners < RING:
                pl.when(pa >= self.owners)(body)

        def arrived(self, sem, region):
            remote(region, region, self.send.at[0], sem, partner).wait_recv()

        def left(self, which, tiles):
            region = gsum_ref.at[pl.ds(0, tiles)]
            remote(region, region, self.send.at[which], self.recv.at[0], partner).wait_send()

        def pair_sum(self, at, count):
            own = g32[pl.ds(mine + self.at + at, count)]
            return own + self.rc[pl.ds(at, count)].astype(F32)

        def core_start(self):
            remote(g16.at[pl.ds(theirs + self.at, self.count)], self.rc, self.send.at[0],
                   self.recv.at[0], partner).start()

        def scatter(self):
            self.arrived(self.recv.at[0], self.rc)
            self.s16[...] = self.pair_sum(0, self.count).astype(BF16)
            for dx in ORDER:
                px = (x + dx) % NX

                def body(i, carry):
                    p = (pa + RING // 2 + i) % RING

                    def start():
                        remote(self.s16.at[pl.ds((px * self.owners + p) * self.t, self.t)],
                               self.r1.at[(NX - dx) % NX * RING + pa], self.send.at[0],
                               self.recv.at[1], on_plane(px, p)).start()

                    if dx == 0:
                        pl.when((p < self.owners) & (p != pa))(start)
                    elif self.owners < RING:
                        pl.when(p < self.owners)(start)
                    else:
                        start()
                    return carry

                lax.fori_loop(0, RING, body, 0)

        def swap(self):
            def body():
                t = self.t
                self.arrived(self.recv.at[1], self.r1.at[pl.ds(1, NX * RING - 1)])
                self.r1[pa] = jnp.zeros((t, 16, C1), BF16)
                total = self.pair_sum((x * self.owners + pa) * t, t)
                for s in range(NX * RING):
                    total = total + self.r1[s].astype(F32)
                self.e[0] = total.astype(BF16)

                def start(s, carry):
                    remote(self.e.at[0], self.e.at[s], self.send.at[0], self.recv.at[2],
                           on_b((pb + s) % RING)).start()
                    return carry

                lax.fori_loop(1, RING, start, 0)

            self.when_owner(body)

        def region(self, px, p, owners):
            return gsum_ref.at[pl.ds(mine + self.at + px * self.group + p * self.t, owners * self.t)]

        def gather(self):
            def body():
                self.arrived(self.recv.at[2], self.e.at[pl.ds(1, RING - 1)])
                total = self.e[pb % RING].astype(F32)
                for p in range(1, RING):
                    total = total + self.e[(pb - p + RING) % RING].astype(F32)
                own = self.region(x, pa, 1)
                own[...] = total.astype(BF16)
                for dx in ORDER:

                    def start(i, carry):
                        p = (pa + RING // 2 + i) % RING

                        def go():
                            remote(own, own, self.send.at[1], self.late.at[(NX - dx) % NX],
                                   on_plane((x + dx) % NX, p)).start()

                        if dx == 0:
                            pl.when(p != pa)(go)
                        else:
                            go()
                        return carry

                    lax.fori_loop(0, RING, start, 0)

            self.when_owner(body)

        def pass_on(self, g):
            px = (x + g) % NX
            whole = self.region(px, 0, self.owners)
            if g == 0:
                self.when_owner(
                    lambda: self.arrived(self.late.at[0], self.region(px, 0, self.owners - 1))
                )
                self.unless_owner(lambda: self.arrived(self.late.at[0], whole))
            else:
                self.arrived(self.late.at[g], whole)
            remote(whole, whole, self.send.at[1], self.recv.at[3], partner).start()

        def finish(self):
            self.arrived(self.recv.at[3], gsum_ref.at[pl.ds(theirs + self.at, self.count)])
            t, others = self.t, NX * RING - 1

            def owner():
                self.left(0, self.count + (NX * self.owners - 1 + RING - 1) * t)
                self.left(1, self.count + others * t)

            def rest():
                self.left(0, self.count + NX * self.owners * t)
                self.left(1, self.count)

            self.when_owner(owner)
            self.unless_owner(rest)

    down, sub = [Part(i) for i in range(2)]

    grad_down = lax.dot_general(
        kids_ref[...], seeded, (((0,), (0,)), ((), ())), preferred_element_type=F32
    )
    put(SUB, grad_down[:, :C1])
    put(HALF + SUB, grad_down[:, C1:])
    down.core_start()

    slope = sig * (1.0 + preact * (1.0 - sig))
    pre_grad = (hidden_grad * slope * mask).astype(BF16).astype(F32)
    stage_halo(1, pre_grad)
    send_halo(1)
    turned = pre_grad.T.astype(BF16)

    def put_sub(k):
        block = jnp.dot(
            turned, cols_ref[:, k * C1 : (k + 1) * C1], preferred_element_type=F32
        ).T
        if k < 13:
            put(8 * k, block)
        elif k == 13:
            put(8 * k, block[:64])
            put(HALF, block[64:])
        else:
            put(HALF + 8 * k - 108, block)

    for k in range(20):
        put_sub(k)
    down.scatter()
    for k in range(20, 27):
        put_sub(k)
    if SUB > 108:
        for h in range(2):
            put(h * HALF + 108, jnp.zeros(((SUB - 108) * 16, C1), F32))
    sub.core_start()
    center(pre_grad)
    output = jnp.dot(kids_ref[...], wdown_ref[...], preferred_element_type=F32)
    out_ref[...] = (output * coarse).astype(BF16)
    sub.scatter()

    whole_halo(1).wait_recv()
    columns(1)
    gfeat = lax.dot_general(
        cols_ref[...], wflip_ref[...], (((1,), (1,)), ((), ())), preferred_element_type=F32
    )
    gfeat_ref[...] = (gfeat * mask_ref[...]).astype(BF16)

    down.swap()
    sub.swap()
    down.gather()
    sub.gather()
    for part in (down, sub):
        for g in reversed(ORDER):
            part.pass_on(g)
    down.finish()
    sub.finish()
    for which in range(2):
        whole_halo(which).wait_send()


def finish_kernel(
    scale, sums, output_in, gfeat_in, output, gfeat, gsub, gdown,
    sums_ref, output_ref, gfeat_ref, sub_ref, down_ref, in_sem, out_sem,
):
    cuts = ((0, 54), (54, 108), (SUB, HALF))
    loads = {}
    for h in range(2):
        for i, (low, high) in enumerate(cuts):
            region = pl.ds(h * HALF + low, high - low)
            loads[h, i] = pltpu.make_async_copy(sums.at[region], sums_ref.at[region], in_sem.at[h, i])
    for piece in ((0, 0), (0, 1), (1, 0), (1, 1), (0, 2), (1, 2)):
        loads[piece].start()
    small = [
        pltpu.make_async_copy(output_in, output_ref, out_sem.at[0]),
        pltpu.make_async_copy(gfeat_in, gfeat_ref, out_sem.at[1]),
    ]
    for load in small:
        load.start()
    copies = []

    def widened(h, i):
        low, high = cuts[i]
        return (sums_ref[h * HALF + low : h * HALF + high].astype(F32) * scale).reshape(-1, C1)

    def store(src, dst):
        copies.append(pltpu.make_async_copy(src, dst, out_sem.at[2 + len(copies)]))
        copies[-1].start()

    for h in range(2):
        for i in range(2):
            loads[h, i].wait()
            rows = pl.ds((h * 108 + cuts[i][0]) * 16, 54 * 16)
            sub_ref[rows] = widened(h, i)
            store(sub_ref.at[rows], gsub.at[rows])
    for h in range(2):
        loads[h, 2].wait()
        down_ref[:, h * C1 : (h + 1) * C1] = widened(h, 2)
    for r in range(2):
        rows = pl.ds(r * 512, 512)
        store(down_ref.at[rows], gdown.at[rows])
    for load in small:
        load.wait()
    store(output_ref, output)
    store(gfeat_ref, gfeat)
    for copy in copies:
        copy.wait()


def local(features, occupancy, neighbours, weight_sub, weight_down, cotangent):
    def tiles(*shape):
        return pltpu.VMEM(shape + (16, C1), BF16)

    vmem, any_space = pl.BlockSpec(memory_space=pltpu.VMEM), pl.BlockSpec(memory_space=pl.ANY)
    dma = pltpu.SemaphoreType.DMA
    part_scratch = []
    for _, owners, t in PARTS:
        count = NX * owners * t
        part_scratch += [
            tiles(count), tiles(count), tiles(NX * RING, t), tiles(RING, t),
            dma((2,)), dma((4,)), dma((NX,)),
        ]
    output, grad_features, sums = pl.pallas_call(
        kernel,
        out_shape=(
            jax.ShapeDtypeStruct((64, C2), BF16),
            jax.ShapeDtypeStruct((V, C1), BF16),
            jax.ShapeDtypeStruct((2 * HALF, 16, C1), BF16),
        ),
        in_specs=[any_space] * 6,
        out_specs=(vmem, vmem, vmem),
        scratch_shapes=[
            pltpu.SMEM((1, 27), jnp.int32),
            pltpu.VMEM((V, C1), BF16),
            pltpu.VMEM((1, V), jnp.int32),
            pltpu.VMEM((27 * C1, C1), BF16),
            pltpu.VMEM((8 * C1, C2), BF16),
            pltpu.VMEM((64, C2), BF16),
            pltpu.VMEM((V, C1), F32),
            pltpu.VMEM((V, C1), F32),
            pltpu.VMEM((3, 10, 10, 8, C1), F32),
            pltpu.VMEM((V, 27 * C1), BF16),
            pltpu.VMEM((C1, 27 * C1), BF16),
            pltpu.VMEM((64, 8 * C1), BF16),
            tiles(2, 20), tiles(2, 20),
            pltpu.VMEM((2 * HALF, 16, C1), F32),
            tiles(2 * HALF),
            dma((6,)), dma((2,)), dma((2,)),
        ] + part_scratch,
        compiler_params=pltpu.CompilerParams(
            collective_id=0, has_side_effects=True, vmem_limit_bytes=60 * 1024 * 1024
        ),
    )(
        neighbours.reshape(1, 27),
        features.reshape(V, C1),
        occupancy.reshape(1, V),
        weight_sub.reshape(27 * C1, C1),
        weight_down.reshape(8 * C1, C2),
        cotangent.reshape(64, C2),
    )
    scale = 1.0 / math.sqrt(lax.axis_size("gx") * lax.axis_size("gy") * V)
    output, grad_features, grad_sub, grad_down = pl.pallas_call(
        functools.partial(finish_kernel, scale),
        out_shape=(
            jax.ShapeDtypeStruct((64, C2), BF16),
            jax.ShapeDtypeStruct((V, C1), BF16),
            jax.ShapeDtypeStruct((27 * C1, C1), F32),
            jax.ShapeDtypeStruct((8 * C1, C2), F32),
        ),
        in_specs=[any_space] * 3,
        out_specs=(any_space,) * 4,
        scratch_shapes=[
            tiles(2 * HALF), pltpu.VMEM((64, C2), BF16), pltpu.VMEM((V, C1), BF16),
            pltpu.VMEM((27 * C1, C1), F32), pltpu.VMEM((8 * C1, C2), F32), dma((2, 3)), dma((10,)),
        ],
        compiler_params=pltpu.CompilerParams(vmem_limit_bytes=60 * 1024 * 1024),
    )(sums, output, grad_features)
    return (
        output.reshape(1, 1, 1, 64, C2),
        grad_features.reshape(1, 1, 1, V, C1),
        grad_sub.reshape(27, C1, C1),
        grad_down.reshape(8, C1, C2),
    )


def solution(mesh):
    return jax.shard_map(
        local,
        mesh=mesh,
        in_specs=(
            P("gx", "gy", None, None, None),
            P("gx", "gy", None, None),
            P("gx", "gy", None, None),
            P(),
            P(),
            P("gx", "gy", None, None, None),
        ),
        out_specs=(P("gx", "gy", None, None, None), P("gx", "gy", None, None, None), P(), P()),
        check_vma=False,
    )
```

time: 68.9 us -> 60 us (0.87)
  local copies, waits for them, and re-layouts: 6.54 us -> 0 us
  other arithmetic: 2.44 us -> 0 us
    unnamed x14 -> x0, local copies, waits for them, and re-layouts: 6.47 us -> none
    pallas_call x0 -> x1, Pallas kernels: none -> 2.7 us  [local(): pl.pallas_call(functools.partial(finish_kernel, scale), out_shape=(jax.Sh...]
    pallas_call x1, Pallas kernels: 58.9 us -> 56.5 us  [local(): pl.pallas_call(kernel, out_shape=(jax.ShapeDtypeStruct((64, C2), BF16), j...]
    mul x2 -> x0, other arithmetic: 1.39 us -> none  [the longest x1 1.32 us: local(): grad_sub = sums[:216].reshape(27, C1, C1).astype(F32) * scale]
    concatenate x1 -> x0, other arithmetic: 1.04 us -> none  [local(): jnp.concatenate([grad_down[0], grad_down[1]], axis=2)]
where the time goes in v2:
time: 60 us; the launch traced here: 59.8 us
  Pallas kernels  59.2 us (99%)
  between operations  0.64 us (1%)
    pallas_call x1, Pallas kernels, local(): pl.pallas_call(kernel, out_shape=(jax.ShapeDtypeStruct((64, C2), BF16), j...  56.5 us
    pallas_call x1, Pallas kernels, local(): pl.pallas_call(functools.partial(finish_kernel, scale), out_shape=(jax.Sh...  2.7 us

profile of v2, /device:TPU:1, one launch (start us, length us, event | category | flops | bytes accessed | tf_op | source)
XLA Modules:
  0.0 59.8 jit_solution(17916933381067899039)
XLA Ops:
  0.6 56.5 %shard_map.93 = (bf16[64,256]{1,0:T(8,128)(2,1)}, bf16[512,128]{1,0:T(8,128)(2,1)}, bf16[352,16,128]{2,1,0:T(8,128)(2,1)}) custom-call(s32[1,27]{1,0:T(1,128)} %bitcast.15, bf16[512,128]{1,0:T(8,128)(2,1)} %bitcast.12, s32[1,512]{1,0:T(1,128)} %bitcast.14, bf16[3456,128]{1,0:T(8,128)(2,1)} %bitcast.10, bf16[1024,256]{1,0:T(8,128)(2,1)} %bitcast.11, ...), custom_call_target="tpu_custom_call" | custom-call | tf_op jit(solution)/shard_map/pallas_call | solution.py:505
  57.1 2.7 %shard_map.94 = (bf16[64,256]{1,0:T(8,128)(2,1)}, bf16[512,128]{1,0:T(8,128)(2,1)}, f32[3456,128]{1,0:T(8,128)}, f32[1024,256]{1,0:T(8,128)}) custom-call(bf16[352,16,128]{2,1,0:T(8,128)(2,1)} %get-tuple-element.11.sums, bf16[64,256]{1,0:T(8,128)(2,1)} %get-tuple-element.12.output_in, bf16[512,128]{1,0:T(8,128)(2,1)} %get-tuple-element.13.gfeat_in), custom_call_target="tpu_custom_call" | custom-call | tf_op jit(solution)/shard_map/pallas_call | solution.py:544

commit v3 on v2

--- a/solution.py
+++ b/solution.py
@@ -16,11 +16,16 @@
 NX = X_LO * X_HI
 
 SUB_OWNERS = RING - 1
-SUB_T = -(-108 // (NX * SUB_OWNERS))
-SUB = NX * SUB_OWNERS * SUB_T
+SUB_T = -(-108 // (2 * NX * SUB_OWNERS))
+SUB_PART = NX * SUB_OWNERS * SUB_T
+SUB = 2 * SUB_PART
 HALF = SUB + 64
 ORDER = (2, 1, 3, 0) if NX == 4 else (1, 0)
-PARTS = ((SUB, RING, 64 // (NX * RING)), (0, SUB_OWNERS, SUB_T))
+PARTS = (
+    (SUB, RING, 64 // (NX * RING)),
+    (0, SUB_OWNERS, SUB_T),
+    (SUB_PART, SUB_OWNERS, SUB_T),
+)
 
 
 FACES = ((1, 0), (-1, 0), (0, 1), (0, -1))
@@ -57,8 +62,6 @@
             )
         )
     ]
-    for load in loads:
-        load.start()
     gx, gy = lax.axis_index("gx"), lax.axis_index("gy")
     core = gx % 2
     y = (gx // 2) % RING
@@ -90,6 +93,8 @@
 
     for dx, dy in FACES + EDGES:
         greet(tile_at(dx, dy))
+    for load in loads:
+        load.start()
     greet(partner)
 
     def greet_plane(i, carry):
@@ -380,7 +385,7 @@
             self.when_owner(owner)
             self.unless_owner(rest)
 
-    down, sub = [Part(i) for i in range(2)]
+    down, sub1, sub2 = [Part(i) for i in range(3)]
 
     grad_down = lax.dot_general(
         kids_ref[...], seeded, (((0,), (0,)), ((), ())), preferred_element_type=F32
@@ -395,31 +400,35 @@
     send_halo(1)
     turned = pre_grad.T.astype(BF16)
 
-    def put_sub(k):
-        block = jnp.dot(
-            turned, cols_ref[:, k * C1 : (k + 1) * C1], preferred_element_type=F32
-        ).T
-        if k < 13:
-            put(8 * k, block)
-        elif k == 13:
-            put(8 * k, block[:64])
-            put(HALF, block[64:])
-        else:
-            put(HALF + 8 * k - 108, block)
-
-    for k in range(20):
-        put_sub(k)
+    def put_sub(low, high):
+        blocks = jnp.dot(
+            turned, cols_ref[:, low * C1 : high * C1], preferred_element_type=F32
+        )
+        for k in range(low, high):
+            block = blocks[:, (k - low) * C1 : (k - low + 1) * C1].T
+            if k < 13:
+                put(8 * k, block)
+            elif k == 13:
+                put(8 * k, block[:64])
+                put(HALF, block[64:])
+            else:
+                put(HALF + 8 * k - 108, block)
+
+    first = -(-SUB_PART // 8)
+    second = -(-(108 + SUB_PART) // 8)
+    put_sub(0, first)
+    put_sub(13, second)
+    sub1.core_start()
     down.scatter()
-    for k in range(20, 27):
-        put_sub(k)
+    put_sub(first, 13)
+    put_sub(second, 27)
     if SUB > 108:
         for h in range(2):
             put(h * HALF + 108, jnp.zeros(((SUB - 108) * 16, C1), F32))
-    sub.core_start()
+    sub2.core_start()
+    sub1.scatter()
     center(pre_grad)
-    output = jnp.dot(kids_ref[...], wdown_ref[...], preferred_element_type=F32)
-    out_ref[...] = (output * coarse).astype(BF16)
-    sub.scatter()
+    sub2.scatter()
 
     whole_halo(1).wait_recv()
     columns(1)
@@ -427,62 +436,46 @@
         cols_ref[...], wflip_ref[...], (((1,), (1,)), ((), ())), preferred_element_type=F32
     )
     gfeat_ref[...] = (gfeat * mask_ref[...]).astype(BF16)
-
-    down.swap()
-    sub.swap()
-    down.gather()
-    sub.gather()
-    for part in (down, sub):
+    output = jnp.dot(kids_ref[...], wdown_ref[...], preferred_element_type=F32)
+    out_ref[...] = (output * coarse).astype(BF16)
+
+    parts = (down, sub1, sub2)
+    for part in parts:
+        part.swap()
+    for part in parts:
+        part.gather()
+    for part in parts:
         for g in reversed(ORDER):
             part.pass_on(g)
-    down.finish()
-    sub.finish()
+    for part in parts:
+        part.finish()
     for which in range(2):
         whole_halo(which).wait_send()
 
 
 def finish_kernel(
-    scale, sums, output_in, gfeat_in, output, gfeat, gsub, gdown,
-    sums_ref, output_ref, gfeat_ref, sub_ref, down_ref, in_sem, out_sem,
+    scale, sums_ref, output_ref, gfeat_ref, output, gfeat, gsub, gdown, sub_ref, down_ref, sem
 ):
-    cuts = ((0, 54), (54, 108), (SUB, HALF))
-    loads = {}
+    copies = []
+
+    def store(src, dst):
+        copies.append(pltpu.make_async_copy(src, dst, sem.at[len(copies)]))
+        copies[-1].start()
+
+    def widened(low, high):
+        return (sums_ref[low:high].astype(F32) * scale).reshape(-1, C1)
+
     for h in range(2):
-        for i, (low, high) in enumerate(cuts):
-            region = pl.ds(h * HALF + low, high - low)
-            loads[h, i] = pltpu.make_async_copy(sums.at[region], sums_ref.at[region], in_sem.at[h, i])
-    for piece in ((0, 0), (0, 1), (1, 0), (1, 1), (0, 2), (1, 2)):
-        loads[piece].start()
-    small = [
-        pltpu.make_async_copy(output_in, output_ref, out_sem.at[0]),
-        pltpu.make_async_copy(gfeat_in, gfeat_ref, out_sem.at[1]),
-    ]
-    for load in small:
-        load.start()
-    copies = []
-
-    def widened(h, i):
-        low, high = cuts[i]
-        return (sums_ref[h * HALF + low : h * HALF + high].astype(F32) * scale).reshape(-1, C1)
-
-    def store(src, dst):
-        copies.append(pltpu.make_async_copy(src, dst, out_sem.at[2 + len(copies)]))
-        copies[-1].start()
-
-    for h in range(2):
-        for i in range(2):
-            loads[h, i].wait()
-            rows = pl.ds((h * 108 + cuts[i][0]) * 16, 54 * 16)
-            sub_ref[rows] = widened(h, i)
+        for i in range(3):
+            rows = pl.ds((h * 108 + i * 36) * 16, 36 * 16)
+            sub_ref[rows] = widened(h * HALF + i * 36, h * HALF + i * 36 + 36)
             store(sub_ref.at[rows], gsub.at[rows])
-    for h in range(2):
-        loads[h, 2].wait()
-        down_ref[:, h * C1 : (h + 1) * C1] = widened(h, 2)
     for r in range(2):
         rows = pl.ds(r * 512, 512)
+        for h in range(2):
+            low = h * HALF + SUB + r * 32
+            down_ref[rows, h * C1 : (h + 1) * C1] = widened(low, low + 32)
         store(down_ref.at[rows], gdown.at[rows])
-    for load in small:
-        load.wait()
     store(output_ref, output)
     store(gfeat_ref, gfeat)
     for copy in copies:
@@ -505,12 +498,10 @@
     output, grad_features, sums = pl.pallas_call(
         kernel,
         out_shape=(
-            jax.ShapeDtypeStruct((64, C2), BF16),
-            jax.ShapeDtypeStruct((V, C1), BF16),
-            jax.ShapeDtypeStruct((2 * HALF, 16, C1), BF16),
+            pltpu.VMEM((64, C2), BF16), pltpu.VMEM((V, C1), BF16), tiles(2 * HALF),
         ),
         in_specs=[any_space] * 6,
-        out_specs=(vmem, vmem, vmem),
+        out_specs=(vmem,) * 3,
         scratch_shapes=[
             pltpu.SMEM((1, 27), jnp.int32),
             pltpu.VMEM((V, C1), BF16),
@@ -530,15 +521,20 @@
             dma((6,)), dma((2,)), dma((2,)),
         ] + part_scratch,
         compiler_params=pltpu.CompilerParams(
-            collective_id=0, has_side_effects=True, vmem_limit_bytes=60 * 1024 * 1024
+            collective_id=0, has_side_effects=True, vmem_limit_bytes=40 * 1024 * 1024
         ),
     )(
-        neighbours.reshape(1, 27),
-        features.reshape(V, C1),
-        occupancy.reshape(1, V),
-        weight_sub.reshape(27 * C1, C1),
-        weight_down.reshape(8 * C1, C2),
-        cotangent.reshape(64, C2),
+        *(
+            pltpu.with_memory_space_constraint(arg, pltpu.HBM)
+            for arg in (
+                neighbours.reshape(1, 27),
+                features.reshape(V, C1),
+                occupancy.reshape(1, V),
+                weight_sub.reshape(27 * C1, C1),
+                weight_down.reshape(8 * C1, C2),
+                cotangent.reshape(64, C2),
+            )
+        )
     )
     scale = 1.0 / math.sqrt(lax.axis_size("gx") * lax.axis_size("gy") * V)
     output, grad_features, grad_sub, grad_down = pl.pallas_call(
@@ -549,13 +545,12 @@
             jax.ShapeDtypeStruct((27 * C1, C1), F32),
             jax.ShapeDtypeStruct((8 * C1, C2), F32),
         ),
-        in_specs=[any_space] * 3,
+        in_specs=[vmem] * 3,
         out_specs=(any_space,) * 4,
         scratch_shapes=[
-            tiles(2 * HALF), pltpu.VMEM((64, C2), BF16), pltpu.VMEM((V, C1), BF16),
-            pltpu.VMEM((27 * C1, C1), F32), pltpu.VMEM((8 * C1, C2), F32), dma((2, 3)), dma((10,)),
+            pltpu.VMEM((27 * C1, C1), F32), pltpu.VMEM((8 * C1, C2), F32), dma((10,)),
         ],
-        compiler_params=pltpu.CompilerParams(vmem_limit_bytes=60 * 1024 * 1024),
+        compiler_params=pltpu.CompilerParams(vmem_limit_bytes=16 * 1024 * 1024),
     )(sums, output, grad_features)
     return (
         output.reshape(1, 1, 1, 64, C2),

time: 60 us -> 57.3 us (0.955)
  Pallas kernels: 59.2 us -> 56.6 us
    pallas_call x1, Pallas kernels: 56.5 us -> 54.9 us  [local(): pl.pallas_call(kernel, out_shape=(pltpu.VMEM((64, C2), BF16), pltpu.VMEM(...]
    pallas_call x1, Pallas kernels: 2.7 us -> 1.7 us  [local(): pl.pallas_call(functools.partial(finish_kernel, scale), out_shape=(jax.Sh...]
where the time goes in v3:
time: 57.3 us; the launch traced here: 57.2 us
  Pallas kernels  56.6 us (99%)
  between operations  0.64 us (1%)
    pallas_call x1, Pallas kernels, local(): pl.pallas_call(kernel, out_shape=(pltpu.VMEM((64, C2), BF16), pltpu.VMEM(...  54.9 us
    pallas_call x1, Pallas kernels, local(): pl.pallas_call(functools.partial(finish_kernel, scale), out_shape=(jax.Sh...  1.7 us

profile of v3, /device:TPU:1, one launch (start us, length us, event | category | flops | bytes accessed | tf_op | source)
XLA Modules:
  0.0 57.2 jit_solution(7360144247400747806)
XLA Ops:
  0.6 54.9 %shard_map.93 = (bf16[64,256]{1,0:T(8,128)(2,1)S(1)}, bf16[512,128]{1,0:T(8,128)(2,1)S(1)}, bf16[352,16,128]{2,1,0:T(8,128)(2,1)S(1)}) custom-call(s32[1,27]{1,0:T(1,128)} %bitcast.15, bf16[512,128]{1,0:T(8,128)(2,1)} %bitcast.12, s32[1,512]{1,0:T(1,128)} %bitcast.14, bf16[3456,128]{1,0:T(8,128)(2,1)} %bitcast.10, bf16[1024,256]{1,0:T(8,128)(2,1)} %bitcast.11, ...), custom_call_target="tpu_custom_call" | custom-call | tf_op jit(solution)/shard_map/pallas_call | solution.py:498
  55.5 1.7 %shard_map.94 = (bf16[64,256]{1,0:T(8,128)(2,1)}, bf16[512,128]{1,0:T(8,128)(2,1)}, f32[3456,128]{1,0:T(8,128)}, f32[1024,256]{1,0:T(8,128)}) custom-call(bf16[352,16,128]{2,1,0:T(8,128)(2,1)S(1)} %get-tuple-element.11.sums_ref, bf16[64,256]{1,0:T(8,128)(2,1)S(1)} %get-tuple-element.12.output_ref, bf16[512,128]{1,0:T(8,128)(2,1)S(1)} %get-tuple-element.13.gfeat_ref), custom_call_target="tpu_custom_call" | custom-call | tf_op jit(solution)/shard_map/pallas_call | solution.py:540

commit v4 on v3

--- a/solution.py
+++ b/solution.py
@@ -15,17 +15,17 @@
 X_LO, X_HI, RING = 2, 2, 8
 NX = X_LO * X_HI
 
+DOWN_PARTS, SUB_PARTS = 1, 2
 SUB_OWNERS = RING - 1
-SUB_T = -(-108 // (2 * NX * SUB_OWNERS))
+SUB_T = -(-108 // (SUB_PARTS * NX * SUB_OWNERS))
 SUB_PART = NX * SUB_OWNERS * SUB_T
-SUB = 2 * SUB_PART
+SUB = SUB_PARTS * SUB_PART
+DOWN_PART = 64 // DOWN_PARTS
 HALF = SUB + 64
 ORDER = (2, 1, 3, 0) if NX == 4 else (1, 0)
-PARTS = (
-    (SUB, RING, 64 // (NX * RING)),
-    (0, SUB_OWNERS, SUB_T),
-    (SUB_PART, SUB_OWNERS, SUB_T),
-)
+PARTS = [
+    (SUB + i * DOWN_PART, RING, DOWN_PART // (NX * RING)) for i in range(DOWN_PARTS)
+] + [(i * SUB_PART, SUB_OWNERS, SUB_T) for i in range(SUB_PARTS)]
 
 
 FACES = ((1, 0), (-1, 0), (0, 1), (0, -1))
@@ -86,28 +86,33 @@
     def tile_at(dx, dy):
         return ((gx + dx + tiles_x) % tiles_x, (gy + dy + tiles_y) % tiles_y)
 
+    places = [(pa + d) % RING for d in range(RING)]
     barrier = pltpu.get_barrier_semaphore()
 
     def greet(target):
         pl.semaphore_signal(barrier, inc=1, device_id=target, device_id_type=MESH)
 
+    row = [jnp.where(core == 0, p, y) * 2 + core for p in places]
+    column = [jnp.where(core == 0, z, p) * X_HI for p in places]
+    x_low = [((x + dx) % NX) % X_LO * (2 * RING) for dx in range(NX)]
+    x_high = [((x + dx) % NX) // X_LO for dx in range(NX)]
+    plane = [(dx, d) for dx in range(NX) for d in range(RING) if dx or d]
+    plane.sort(key=lambda step: -min(step[0], NX - step[0]) - min(step[1], RING - step[1]))
+
+    def greet_plane(steps):
+        for dx, d in steps:
+            greet((x_low[dx] + row[d], column[d] + x_high[dx]))
+
+    far = len(plane) * 2 // 5
+    greet_plane(plane[:far])
     for dx, dy in FACES + EDGES:
         greet(tile_at(dx, dy))
+    for d in range(1, RING):
+        greet(on_b((pb + d) % RING))
+    greet_plane(plane[far:])
+    greet(partner)
     for load in loads:
         load.start()
-    greet(partner)
-
-    def greet_plane(i, carry):
-        greet(on_plane((x + i // RING) % NX, (pa + i) % RING))
-        return carry
-
-    lax.fori_loop(1, NX * RING, greet_plane, 0)
-
-    def greet_ring(s, carry):
-        greet(on_b((pb + s) % RING))
-        return carry
-
-    lax.fori_loop(1, RING, greet_ring, 0)
 
     def remote(src, dst, send, recv, target):
         return pltpu.make_async_remote_copy(
@@ -385,19 +390,19 @@
             self.when_owner(owner)
             self.unless_owner(rest)
 
-    down, sub1, sub2 = [Part(i) for i in range(3)]
+    parts = [Part(i) for i in range(DOWN_PARTS + SUB_PARTS)]
+    split = DOWN_PARTS + SUB_PARTS // 2
 
     grad_down = lax.dot_general(
         kids_ref[...], seeded, (((0,), (0,)), ((), ())), preferred_element_type=F32
     )
     put(SUB, grad_down[:, :C1])
     put(HALF + SUB, grad_down[:, C1:])
-    down.core_start()
+    for part in parts[:DOWN_PARTS]:
+        part.core_start()
 
     slope = sig * (1.0 + preact * (1.0 - sig))
     pre_grad = (hidden_grad * slope * mask).astype(BF16).astype(F32)
-    stage_halo(1, pre_grad)
-    send_halo(1)
     turned = pre_grad.T.astype(BF16)
 
     def put_sub(low, high):
@@ -414,22 +419,31 @@
             else:
                 put(HALF + 8 * k - 108, block)
 
-    first = -(-SUB_PART // 8)
-    second = -(-(108 + SUB_PART) // 8)
+    early = SUB_PARTS // 2 * SUB_PART
+    first = -(-early // 8)
+    second = -(-(108 + early) // 8)
     put_sub(0, first)
     put_sub(13, second)
-    sub1.core_start()
-    down.scatter()
+    for part in parts[DOWN_PARTS:split]:
+        part.core_start()
     put_sub(first, 13)
     put_sub(second, 27)
     if SUB > 108:
         for h in range(2):
             put(h * HALF + 108, jnp.zeros(((SUB - 108) * 16, C1), F32))
-    sub2.core_start()
-    sub1.scatter()
+    for part in parts[split:]:
+        part.core_start()
+    for part in parts:
+        part.scatter()
+    stage_halo(1, pre_grad)
+    send_halo(1)
+
+    for part in parts:
+        part.swap()
+    for part in parts:
+        part.gather()
+
     center(pre_grad)
-    sub2.scatter()
-
     whole_halo(1).wait_recv()
     columns(1)
     gfeat = lax.dot_general(
@@ -439,13 +453,8 @@
     output = jnp.dot(kids_ref[...], wdown_ref[...], preferred_element_type=F32)
     out_ref[...] = (output * coarse).astype(BF16)
 
-    parts = (down, sub1, sub2)
     for part in parts:
-        part.swap()
-    for part in parts:
-        part.gather()
-    for part in parts:
-        for g in reversed(ORDER):
+        for g in ORDER:
             part.pass_on(g)
     for part in parts:
         part.finish()

time: 57.3 us -> 56 us (0.977)
  Pallas kernels: 56.6 us -> 55.2 us
    pallas_call x1, Pallas kernels: 54.9 us -> 53.5 us  [local(): pl.pallas_call(kernel, out_shape=(pltpu.VMEM((64, C2), BF16), pltpu.VMEM(...]
where the time goes in v4:
time: 56 us; the launch traced here: 55.9 us
  Pallas kernels  55.2 us (99%)
  between operations  0.64 us (1%)
    pallas_call x1, Pallas kernels, local(): pl.pallas_call(kernel, out_shape=(pltpu.VMEM((64, C2), BF16), pltpu.VMEM(...  53.5 us
    pallas_call x1, Pallas kernels, local(): pl.pallas_call(functools.partial(finish_kernel, scale), out_shape=(jax.Sh...  1.7 us

profile of v4, /device:TPU:1, one launch (start us, length us, event | category | flops | bytes accessed | tf_op | source)
XLA Modules:
  0.0 55.9 jit_solution(12204874160892465979)
XLA Ops:
  0.6 53.5 %shard_map.93 = (bf16[64,256]{1,0:T(8,128)(2,1)S(1)}, bf16[512,128]{1,0:T(8,128)(2,1)S(1)}, bf16[352,16,128]{2,1,0:T(8,128)(2,1)S(1)}) custom-call(s32[1,27]{1,0:T(1,128)} %bitcast.15, bf16[512,128]{1,0:T(8,128)(2,1)} %bitcast.12, s32[1,512]{1,0:T(1,128)} %bitcast.14, bf16[3456,128]{1,0:T(8,128)(2,1)} %bitcast.10, bf16[1024,256]{1,0:T(8,128)(2,1)} %bitcast.11, ...), custom_call_target="tpu_custom_call" | custom-call | tf_op jit(solution)/shard_map/pallas_call | solution.py:507
  54.2 1.7 %shard_map.94 = (bf16[64,256]{1,0:T(8,128)(2,1)}, bf16[512,128]{1,0:T(8,128)(2,1)}, f32[3456,128]{1,0:T(8,128)}, f32[1024,256]{1,0:T(8,128)}) custom-call(bf16[352,16,128]{2,1,0:T(8,128)(2,1)S(1)} %get-tuple-element.11.sums_ref, bf16[64,256]{1,0:T(8,128)(2,1)S(1)} %get-tuple-element.12.output_ref, bf16[512,128]{1,0:T(8,128)(2,1)S(1)} %get-tuple-element.13.gfeat_ref), custom_call_target="tpu_custom_call" | custom-call | tf_op jit(solution)/shard_map/pallas_call | solution.py:549

commit v5 on v4

--- a/solution.py
+++ b/solution.py
@@ -105,10 +105,11 @@
 
     far = len(plane) * 2 // 5
     greet_plane(plane[:far])
-    for dx, dy in FACES + EDGES:
+    for dx, dy in EDGES + FACES:
         greet(tile_at(dx, dy))
+    ring = [on_b((pb + d) % RING) for d in range(RING)]
     for d in range(1, RING):
-        greet(on_b((pb + d) % RING))
+        greet(ring[d])
     greet_plane(plane[far:])
     greet(partner)
     for load in loads:
@@ -121,12 +122,12 @@
         )
 
     def send_halo(which):
-        for d, (dx, dy) in enumerate(FACES):
-            region = pl.ds(4 * d, 4)
+        for d, (dx, dy) in enumerate(EDGES):
+            region = pl.ds(16 + d, 1)
             remote(shalo.at[which, region], rhalo.at[which, region], hs_sem.at[which],
                    hr_sem.at[which], tile_at(dx, dy)).start()
-        for d, (dx, dy) in enumerate(EDGES):
-            region = pl.ds(16 + d, 1)
+        for d, (dx, dy) in reversed(list(enumerate(FACES))):
+            region = pl.ds(4 * d, 4)
             remote(shalo.at[which, region], rhalo.at[which, region], hs_sem.at[which],
                    hr_sem.at[which], tile_at(dx, dy)).start()
 
@@ -324,12 +325,9 @@
                     total = total + self.r1[s].astype(F32)
                 self.e[0] = total.astype(BF16)
 
-                def start(s, carry):
+                for s in sorted(range(1, RING), key=lambda s: -min(s, RING - s)):
                     remote(self.e.at[0], self.e.at[s], self.send.at[0], self.recv.at[2],
-                           on_b((pb + s) % RING)).start()
-                    return carry
-
-                lax.fori_loop(1, RING, start, 0)
+                           ring[s]).start()
 
             self.when_owner(body)
 
@@ -474,6 +472,8 @@
     def widened(low, high):
         return (sums_ref[low:high].astype(F32) * scale).reshape(-1, C1)
 
+    store(output_ref, output)
+    store(gfeat_ref, gfeat)
     for h in range(2):
         for i in range(3):
             rows = pl.ds((h * 108 + i * 36) * 16, 36 * 16)
@@ -485,8 +485,6 @@
             low = h * HALF + SUB + r * 32
             down_ref[rows, h * C1 : (h + 1) * C1] = widened(low, low + 32)
         store(down_ref.at[rows], gdown.at[rows])
-    store(output_ref, output)
-    store(gfeat_ref, gfeat)
     for copy in copies:
         copy.wait()
 

time: 56 us -> 55.6 us (level)
  no operation moved by 1% of the time
where the time goes in v5:
time: 55.6 us; the launch traced here: 55.5 us
  Pallas kernels  54.9 us (99%)
  between operations  0.64 us (1%)
    pallas_call x1, Pallas kernels, local(): pl.pallas_call(kernel, out_shape=(pltpu.VMEM((64, C2), BF16), pltpu.VMEM(...  53.2 us
    pallas_call x1, Pallas kernels, local(): pl.pallas_call(functools.partial(finish_kernel, scale), out_shape=(jax.Sh...  1.69 us

profile of v5, /device:TPU:1, one launch (start us, length us, event | category | flops | bytes accessed | tf_op | source)
XLA Modules:
  0.0 55.5 jit_solution(8178019166615306228)
XLA Ops:
  0.6 53.2 %shard_map.93 = (bf16[64,256]{1,0:T(8,128)(2,1)S(1)}, bf16[512,128]{1,0:T(8,128)(2,1)S(1)}, bf16[352,16,128]{2,1,0:T(8,128)(2,1)S(1)}) custom-call(s32[1,27]{1,0:T(1,128)} %bitcast.15, bf16[512,128]{1,0:T(8,128)(2,1)} %bitcast.12, s32[1,512]{1,0:T(1,128)} %bitcast.14, bf16[3456,128]{1,0:T(8,128)(2,1)} %bitcast.10, bf16[1024,256]{1,0:T(8,128)(2,1)} %bitcast.11, ...), custom_call_target="tpu_custom_call" | custom-call | tf_op jit(solution)/shard_map/pallas_call | solution.py:505
  53.8 1.7 %shard_map.94 = (bf16[64,256]{1,0:T(8,128)(2,1)}, bf16[512,128]{1,0:T(8,128)(2,1)}, f32[3456,128]{1,0:T(8,128)}, f32[1024,256]{1,0:T(8,128)}) custom-call(bf16[352,16,128]{2,1,0:T(8,128)(2,1)S(1)} %get-tuple-element.11.sums_ref, bf16[64,256]{1,0:T(8,128)(2,1)S(1)} %get-tuple-element.12.output_ref, bf16[512,128]{1,0:T(8,128)(2,1)S(1)} %get-tuple-element.13.gfeat_ref), custom_call_target="tpu_custom_call" | custom-call | tf_op jit(solution)/shard_map/pallas_call | solution.py:547
